TPU v7x, 32 devices: a whole 2x2x4 slice. The times are simulated.
32 devices in a mesh: req: 4 (over y, x), tile: 4 (over z), col: 2 (over core).
Axes of the slice: x: 2, y: 2, z: 4, core: 2. Of those that a mesh axis runs over, the one named last changes fastest.
Arguments:
- img_qkv: bfloat16 [4, 64, 64, 3, 1536], P('req', 'tile', None, None, 'col'), may hold values from -10 to 10
- txt_kv: bfloat16 [4, 512, 2, 1536], P('req', 'tile', None, 'col'), may hold values from -8 to 8
- text_len: int32 [4], P('req'), may hold values from 256 to 512, as said below
- hidden_state: bfloat16 [4, 64, 64, 3072], P('req', 'tile', 'col'), may hold values from -3 to 3
- modulation: float32 [28, 4, 3, 3072], P(None, 'req'), may hold values from 0.1 to 1.9
- w_attn_out: bfloat16 [1536, 3072], replicated, may hold values from -0.15625 to 0.15625
- w_final: bfloat16 [3072, 64], replicated, may hold values from -0.109375 to 0.109375
- latent: float32 [4, 64, 64, 64], P('req', 'tile', 'col'), may hold values from -6 to 6
- sigmas: float32 [29], replicated, may hold values from -1 to 3, as said below
- step_index: int32 [1], replicated, may hold values from 0 to 27
- w_preview: float32 [3, 3, 64, 64], replicated, may hold values from -0.25 to 0.25
Outputs:
- velocity: float32 [4, 64, 64, 64], P('req', 'tile', 'col')
- latent_next: float32 [4, 64, 64, 64], P('req', 'tile', 'col')
- preview: float32 [4, 64, 64, 64], P('req', 'tile', 'col')
Inputs may be any that keep to these rules, and one draw needn't show every extreme that they name: `text_len`: some request has exactly 512 live text tokens. sigmas[i] - sigmas[i + 1] lies between 0.1 / 28 and 3.4 / 28.
All inputs are finite; a program needn't handle non-finite values.
Results may differ from a plain program's by a relative error of at most 0.005.
Values may be sent and summed in bfloat16 or wider, within the bound.
A program may use at most 320 MiB of HBM per device.

v0:
```python
import math

import jax
import jax.numpy as jnp
from jax import lax
from jax.sharding import PartitionSpec as P

HD = 128


norm_eps = 1e-06


def padded_2(cells, sides, width):
    for axis, dim in sides:
        count = lax.axis_size(axis)
        ends = count - 1
        head = lax.slice_in_dim(cells, 0, width, axis=dim)
        tail = lax.slice_in_dim(cells, cells.shape[dim] - width, cells.shape[dim], axis=dim)
        cells = jnp.concatenate(
            [
                lax.ppermute(tail, axis, [(i, (i + 1) % count) for i in range(ends)]),
                cells,
                lax.ppermute(head, axis, [((i + 1) % count, i) for i in range(ends)]),
            ],
            axis=dim,
        )
    return cells


def make_fold(queries, img_rows, text_rows, text_limit):
    score_scale = 1.0 / math.sqrt(HD)
    shard_rows = img_rows + text_rows

    def fold_step(carry, piece, start):
        run_max, run_sum, run_acc = carry
        piece_len = piece.shape[0]
        key_index = jnp.arange(piece_len, dtype=jnp.int32)
        in_shard = key_index % shard_rows
        text_pos = key_index // shard_rows * text_rows + in_shard - img_rows
        key_live = (in_shard < img_rows) | (text_pos < text_limit)
        scores = (
            jnp.einsum("qhd,khd->hqk", queries, piece[:, 0], preferred_element_type=jnp.float32)
            * score_scale
        )
        scores = jnp.where(key_live[None, None, :], scores, -1e30)
        new_max = jnp.maximum(run_max, jnp.max(scores, axis=2))
        weights = jnp.where(key_live[None, None, :], jnp.exp(scores - new_max[:, :, None]), 0.0)
        run_sum = jnp.sum(weights, axis=2)
        run_acc = jnp.einsum(
            "hqk,khd->hqd",
            weights.astype(jnp.bfloat16),
            piece[:, 1],
            preferred_element_type=jnp.float32,
        )
        return (new_max, run_sum, run_acc)

    return fold_step


def start_carry(query_rows, head_count):
    return (
        jnp.full((head_count, query_rows), -1e30, jnp.float32),
        jnp.zeros((head_count, query_rows), jnp.float32),
        jnp.zeros((head_count, query_rows, HD), jnp.float32),
    )


def finish(carry):
    run_max, run_sum, run_acc = carry
    return jnp.transpose(run_acc / run_sum[:, :, None], (1, 0, 2)).astype(jnp.bfloat16)


def body(
    img_qkv,
    txt_kv,
    text_len,
    hidden_state,
    modulation,
    w_attn_out,
    w_final,
    latent,
    sigmas,
    step_index,
    w_preview,
):
    tile_rows = img_qkv.shape[1]
    grid_cols = img_qkv.shape[2]
    local_heads = img_qkv.shape[4] // HD
    text_rows = txt_kv.shape[1]
    tile_cols = hidden_state.shape[2]
    col_count = grid_cols // tile_cols
    own_rows = tile_rows * tile_cols
    text_limit = text_len[0]
    all_heads = local_heads * col_count
    img_block = img_qkv[0].reshape(tile_rows, grid_cols, 3, local_heads, HD)
    txt_block = txt_kv[0].reshape(1, text_rows, 2, local_heads, HD)
    img_mixed, txt_mixed = (
        lax.all_to_all(img_block, "col", split_axis=1, concat_axis=3, tiled=True),
        lax.all_to_all(txt_block, "col", split_axis=1, concat_axis=3, tiled=True),
    )
    img_flat = img_mixed.reshape(own_rows, 3, all_heads, HD)
    txt_flat = txt_mixed.reshape(text_rows // col_count, 2, all_heads, HD)
    key_value = jnp.concatenate([img_flat[:, 1:], txt_flat], axis=0)
    fold_step = make_fold(img_flat[:, 0], own_rows, text_rows // col_count, text_limit)
    carry = fold_step(
        start_carry(own_rows, all_heads),
        lax.all_gather(key_value, ("tile", "col"), axis=0, tiled=True),
        jnp.int32(0),
    )
    attended = finish(carry).reshape(own_rows, all_heads * HD)
    branch = jnp.dot(attended, w_attn_out, preferred_element_type=jnp.float32)
    step_now = step_index[0]
    mod_now = lax.dynamic_index_in_dim(modulation, step_now, 0, keepdims=False)[0]
    width = hidden_state.shape[3]
    mixed_state = (
        hidden_state[0].reshape(own_rows, width).astype(jnp.float32) + mod_now[0][None, :] * branch
    )
    row_mean = jnp.mean(mixed_state, axis=1, keepdims=True)
    centred = mixed_state - row_mean
    row_var = jnp.mean(centred * centred, axis=1, keepdims=True)
    normed = (
        centred / jnp.sqrt(row_var + norm_eps) * (1.0 + mod_now[2][None, :]) + mod_now[1][None, :]
    )
    normed = normed.astype(jnp.bfloat16)
    velocity = jnp.dot(normed, w_final, preferred_element_type=jnp.float32)
    channels = velocity.shape[1]
    sigma_step = sigmas[step_now + 1] - sigmas[step_now]
    updated = latent[0].reshape(own_rows, channels) + sigma_step * velocity
    grid_field = updated.reshape(tile_rows, tile_cols, channels)
    padded = padded_2(grid_field, (("tile", 0), ("col", 1)), 1)
    preview = jnp.zeros((tile_rows, tile_cols, channels), jnp.float32)
    for row_off in range(3):
        for col_off in range(3):
            preview = preview + jnp.einsum(
                "yxc,cd->yxd",
                padded[row_off : row_off + tile_rows, col_off : col_off + tile_cols],
                w_preview[row_off, col_off],
                precision=lax.Precision.HIGHEST,
            )
    return (velocity.reshape(1, tile_rows, tile_cols, channels), grid_field[None], preview[None])


def solution(mesh):
    placed = (
        P("req", "tile", None, None, "col"),
        P("req", "tile", None, "col"),
        P("req"),
        P("req", "tile", "col", None),
        P(None, "req", None, None),
        P(),
        P(),
        P("req", "tile", "col", None),
        P(),
        P(),
        P(),
    )
    return jax.shard_map(
        body,
        mesh=mesh,
        in_specs=placed,
        out_specs=(
            P("req", "tile", "col", None),
            P("req", "tile", "col", None),
            P("req", "tile", "col", None),
        ),
        check_vma=False,
    )
```

profile of v0, /device:TPU:0, one launch (start us, length us, event | category | flops | bytes accessed | tf_op | source)
XLA Modules:
  0.0 456.4 jit_solution(9621636207864728363)
XLA Ops:
  7.2 0.0 copy-start
  7.2 10.8 %reshape_squeeze.10 = bf16[16,64,3,6,128]{4,3,1,2,0:T(8,128)(2,1)} reshape(bf16[1,16,64,3,768]{4,2,3,1,0:T(8,128)(2,1)} %param.11) | data formatting | bytes 9437184 | tf_op jit(solution)/shard_map/reshape;squeeze | solution.py:96
  18.0 10.5 %copy.59 = bf16[16,64,3,6,128]{4,0,3,2,1:T(8,128)(2,1)} copy(bf16[16,64,3,6,128]{4,3,1,2,0:T(8,128)(2,1)} %reshape_squeeze.10) | data formatting | bytes 9437184 | tf_op jit(solution)/shard_map/reshape;squeeze | solution.py:96
  28.5 5.9 %all-to-all-start = ((bf16[16,64,3,6,128]{4,0,3,2,1:T(8,128)(2,1)}), bf16[16,64,3,6,128]{4,0,3,2,1:T(8,128)(2,1)}, u32[]{:S(2)}, u32[]{:S(2)}) async-start(bf16[16,64,3,6,128]{4,0,3,2,1:T(8,128)(2,1)} %copy.59), calls=%async_computation | async-start | bytes 9437184 | tf_op jit(solution)/shard_map/all_to_all | solution.py:99
  34.4 0.5 copy.62
  34.9 1.1 copy.63
  36.0 3.3 all-to-all-done
  39.2 4.2 all-to-all-start.1
  43.4 0.0 all-gather.2.cloned.1.call-start
  43.5 4.2 copy.61
  47.6 2.1 copy-done.1
  49.8 0.3 slice.131
  50.1 0.0 copy-start.5
  50.1 1.1 copy.64
  51.2 2.0 pad_maximum_fusion
  53.2 0.0 all-gather.2.cloned.1.call-update
  54.6 1.1 copy.69
  55.7 0.6 fusion.73
  57.6 0.8 dynamic-slice_add_fusion
  58.4 243.5 %all-gather.2.cloned.1.call-done = bf16[4608,2,12,128]{3,0,2,1:T(8,128)(2,1)} async-done(((bf16[576,2,12,128]{3,0,2,1:T(8,128)(2,1)}), bf16[4608,2,12,128]{3,0,2,1:T(8,128)(2,1)}) %all-gather.2.cloned.1.call-update) | async-done | bytes 28311568 | tf_op jit(solution)/shard_map/all_gather | solution.py:108
  301.9 43.7 %bitcast_reduce_fusion = (f32[12,512]{1,0:T(8,128)S(1)}, f32[12,4608,512]{2,1,0:T(8,128)}) fusion(pred[4608]{0:T(1024)(128)(4,1)S(1)} %fusion.67, bf16[512,3,12,128]{3,0,2,1:T(8,128)(2,1)} %bitcast.136, bf16[4608,2,12,128]{3,0,2,1:T(8,128)(2,1)} %all-gather.2.cloned.1.call-done), kind=kOutput, calls=%fused_computation.1 | convolution fusion | flops 7332685824 | bytes 129004032 | tf_op jit(solution)/shard_map/qhd,khd->hqk/dot_general | solution.py:43
  345.6 35.4 %fusion.2 = f32[12,512]{1,0:T(8,128)S(1)} fusion(f32[12,4608,512]{2,1,0:T(8,128)} %get-tuple-element.18, f32[12,512]{1,0:T(8,128)S(1)} %broadcast_maximum_fusion, pred[4608]{0:T(1024)(128)(4,1)S(1)} %fusion.67), kind=kLoop, calls=%fused_computation.5 | loop fusion | flops 141551616 | bytes 113299968 | tf_op jit(solution)/shard_map/reduce_sum | solution.py:49
  381.0 42.5 %fusion.9 = bf16[512,12,128]{0,2,1:T(8,128)(2,1)S(1)} fusion(bf16[4608,2,12,128]{3,0,2,1:T(8,128)(2,1)} %all-gather.2.cloned.1.call-done, f32[12,4608,512]{2,1,0:T(8,128)} %get-tuple-element.18, f32[12,512]{1,0:T(8,128)S(1)} %broadcast_maximum_fusion, pred[4608]{0:T(1024)(128)(4,1)S(1)} %fusion.67, f32[512,12]{0,1:T(8,128)S(1)} %bitcast.148), kind=kOutput, calls=%fused_computation.18 | convolution fusion | flops 7390887936 | bytes 129050624 | tf_op jit(solution)/shard_map/hqk,khd->hqd/dot_general | solution.py:50
  423.5 9.1 %fusion.74 = (f32[512]{0:T(512)S(1)}, f32[512,3072]{1,0:T(8,128)S(1)}) fusion(bf16[512,1536]{0,1:T(8,128)(2,1)S(1)} %bitcast.153, bf16[1536,3072]{1,0:T(8,128)(2,1)} %param.16, f32[3072]{0:T(1024)S(1)} %bitcast.151, bf16[512,3072]{1,0:T(8,128)(2,1)} %bitcast.152), kind=kOutput, calls=%fused_computation.103 | convolution fusion | flops 4838129152 | bytes 20461568 | tf_op jit(solution)/shard_map/dot_general | solution.py:112
  432.6 0.8 multiply_reduce_fusion
  433.3 0.0 copy-start.4
  433.3 1.4 multiply_add_fusion
  434.8 0.1 copy.70
  434.9 0.1 slice_bitcast_fusion.9
  435.0 1.3 collective-permute-start
  436.3 1.3 collective-permute-start.1
  437.6 0.4 fusion.42
  438.0 0.8 copy.68
  438.8 0.1 copy.72
  438.9 0.4 fusion.20
  439.2 2.9 collective-permute-done.1
  442.1 0.1 copy.73
  442.2 1.3 collective-permute-start.2
  443.5 1.3 collective-permute-start.3
  444.8 0.4 fusion.24
  445.2 1.4 collective-permute-done.3
  446.6 0.1 maximum_maximum_fusion
  446.6 0.3 fusion.35
  447.0 0.4 fusion.28
  447.3 0.4 fusion.33
  447.7 0.4 fusion.30
  448.1 0.4 fusion.17
  448.5 1.1 fusion.19
  (17 shorter events, 0.1 us)
Async XLA Ops:
  7.2 426.2 %copy-start = (bf16[3072,64]{0,1:T(8,128)(2,1)S(1)}, bf16[3072,64]{0,1:T(8,128)(2,1)}, u32[]{:S(2)}) copy-start(bf16[3072,64]{0,1:T(8,128)(2,1)} %param.17) | copy-start | bytes 1179652
  28.5 5.9 %copy-start.3 = (bf16[1,128,2,768]{3,2,1,0:T(2,128)(2,1)S(1)}, bf16[1,128,2,768]{3,2,1,0:T(2,128)(2,1)}, u32[]{:S(2)}) copy-start(bf16[1,128,2,768]{3,2,1,0:T(2,128)(2,1)} %param.12) | copy-start | bytes 1179652
  28.5 10.8 %all-to-all-start = ((bf16[16,64,3,6,128]{4,0,3,2,1:T(8,128)(2,1)}), bf16[16,64,3,6,128]{4,0,3,2,1:T(8,128)(2,1)}, u32[]{:S(2)}, u32[]{:S(2)}) async-start(bf16[16,64,3,6,128]{4,0,3,2,1:T(8,128)(2,1)} %copy.59), calls=%async_computation | async-start | bytes 9437184 | tf_op jit(solution)/shard_map/all_to_all | solution.py:99
  39.2 10.8 %all-to-all-start.1 = ((bf16[1,128,2,6,128]{4,2,3,0,1:T(2,128)(2,1)}), bf16[1,128,2,6,128]{4,2,3,0,1:T(2,128)(2,1)}, u32[]{:S(2)}, u32[]{:S(2)}) async-start(bf16[1,128,2,6,128]{4,2,3,0,1:T(2,128)(2,1)} %copy.63), calls=%async_computation.1 | async-start | bytes 786432 | tf_op jit(solution)/shard_map/all_to_all | solution.py:100
  43.4 258.5 %all-gather.2.cloned.1.call-start = ((), (), s32[]{:S(2)}) async-start(), calls=%async_computation.2 | async-start | bytes 31850496 | tf_op jit(solution)/shard_map/all_gather | solution.py:108
  47.6 2.1 copy-start.1
  50.1 5.6 %copy-start.5 = (f32[29]{0:T(128)S(1)}, f32[29]{0:T(128)}, u32[]{:S(2)}) copy-start(f32[29]{0:T(128)} %param.19) | copy-start | bytes 352
  433.3 4.3 copy-start.4
  434.9 14.6 %copy-start.2 = (f32[512,64]{1,0:T(8,128)}, f32[512,64]{1,0:T(8,128)S(1)}, u32[]{:S(2)}) copy-start(f32[512,64]{1,0:T(8,128)S(1)} %copy.70) | copy-start | bytes 393220
  435.0 3.8 collective-permute-start
  436.3 5.8 %collective-permute-start.1 = (f32[1,32,64]{1,2,0:T(8,128)S(1)}, f32[1,32,64]{1,2,0:T(8,128)S(1)}, u32[]{:S(2)}, u32[]{:S(2)}) collective-permute-start(f32[1,32,64]{1,2,0:T(8,128)S(1)} %get-tuple-element.14), channel_id=1, source_target_pairs={{2,0},{4,2},{6,4},{3,1},{5,3},{7,5},{10,8},{12,10},{14,12},{11,9},... | collective-permute-start | bytes 24584 | tf_op jit(solution)/shard_map/ppermute | solution.py:24
  442.2 3.0 collective-permute-start.2
  443.5 3.1 collective-permute-start.3
Sparse Core Ops, SparseCore 0:
  53.4 248.4 all-gather.1
where the time goes:
time: 457 us; the launch traced here: 456 us
  waiting for transfers between devices  251 us (55%)
  matrix products  101 us (22%)
  other arithmetic  39.1 us (9%)
  local copies, waits for them, and re-layouts  33.4 us (7%)
  between operations  17 us (4%)
  starting transfers between devices  15.3 us (3%)
    all_gather x1, waiting for transfers between devices, body(): lax.all_gather(key_value, ('tile', 'col'), axis=0, tiled=True)  244 us
    dot_general x1, matrix products, fold_step(): jnp.einsum('qhd,khd->hqk', queries, piece[:, 0], preferred_element_type=j...  43.7 us
    dot_general x1, matrix products, fold_step(): jnp.einsum('hqk,khd->hqd', weights.astype(jnp.bfloat16), piece[:, 1], pre...  42.5 us
    reduce_sum x1, other arithmetic, fold_step(): run_sum = jnp.sum(weights, axis=2)  35.4 us
    another operation x2, local copies, waits for them, and re-layouts, body(): img_block = img_qkv[0].reshape(tile_rows, grid_cols, 3, local_heads, HD)  21.3 us
  transfers between devices with their start and end apart: 7, of which 4 were waited for; matrix products, arithmetic and copies ran while one was open for 2% of the time, Pallas kernels for 0%

commit v1 on v0

--- a/solution.py
+++ b/solution.py
@@ -1,8 +1,11 @@
+import functools
 import math
 
 import jax
 import jax.numpy as jnp
 from jax import lax
+from jax.experimental import pallas as pl
+from jax.experimental.pallas import tpu as pltpu
 from jax.sharding import PartitionSpec as P
 
 HD = 128
@@ -69,6 +72,163 @@
 def finish(carry):
     run_max, run_sum, run_acc = carry
     return jnp.transpose(run_acc / run_sum[:, :, None], (1, 0, 2)).astype(jnp.bfloat16)
+
+
+def attend_kernel(moves, key_chunk, image_keys, q_ref, bias_ref, *refs):
+    parts = refs[:-3]
+    o_ref, kbuf, vbuf = refs[-3:]
+
+    @pl.when(pl.program_id(0) == 0)
+    def _():
+        vbuf[:, HD:] = jnp.ones((vbuf.shape[0], HD), jnp.bfloat16)
+        for which, block, k_from, v_from, size, to in moves:
+            kbuf[to : to + size, :] = parts[which][block, k_from : k_from + size, :]
+            vbuf[to : to + size, :HD] = parts[which][block, v_from : v_from + size, :]
+
+    factor = math.log2(math.e) / math.sqrt(HD)
+    queries = q_ref[0]
+    all_keys = kbuf.shape[0]
+    pieces = [(at, key_chunk) for at in range(0, image_keys, key_chunk)]
+    pieces.append((image_keys, all_keys - image_keys))
+    run_max = acc = None
+    for at, size in pieces:
+        scores = (
+            lax.dot_general(
+                queries,
+                kbuf[at : at + size, :],
+                (((1,), (1,)), ((), ())),
+                preferred_element_type=jnp.float32,
+            )
+            * factor
+        )
+        if at == image_keys:
+            scores = scores + bias_ref[...]
+        top = jnp.max(scores, axis=1, keepdims=True)
+        new_max = top if run_max is None else jnp.maximum(run_max, top)
+        probs = jnp.exp2(scores - new_max).astype(jnp.bfloat16)
+        term = jnp.dot(probs, vbuf[at : at + size, :], preferred_element_type=jnp.float32)
+        acc = term if acc is None else acc * jnp.exp2(run_max - new_max) + term
+        run_max = new_max
+    o_ref[0] = (acc[:, :HD] / acc[:, HD:]).astype(jnp.bfloat16)
+
+
+def attend(block, others, bias, query_rows, moves, image_keys, q_tile, key_chunk):
+    blocks = block.shape[0]
+    per_block = query_rows // q_tile
+    all_keys = image_keys + bias.shape[1]
+    parts = (block,) + others
+
+    def whole(array):
+        return pl.BlockSpec(array.shape, lambda i: (0,) * array.ndim)
+
+    queries = blocks * query_rows
+    return pl.pallas_call(
+        functools.partial(attend_kernel, moves, key_chunk, image_keys),
+        grid=(blocks * per_block,),
+        out_shape=jax.ShapeDtypeStruct((blocks, query_rows, HD), jnp.bfloat16),
+        in_specs=[
+            pl.BlockSpec((1, q_tile, HD), lambda i: (i // per_block, i % per_block, 0)),
+            whole(bias),
+        ]
+        + [whole(part) for part in parts],
+        out_specs=pl.BlockSpec((1, q_tile, HD), lambda i: (i // per_block, i % per_block, 0)),
+        scratch_shapes=[
+            pltpu.VMEM((all_keys, HD), jnp.bfloat16),
+            pltpu.VMEM((all_keys, 2 * HD), jnp.bfloat16),
+        ],
+        compiler_params=pltpu.CompilerParams(vmem_limit_bytes=48 * 1024 * 1024),
+        cost_estimate=pl.CostEstimate(
+            flops=6 * queries * all_keys * HD,
+            bytes_accessed=2 * sum(part.size for part in parts) + 4 * queries * HD,
+            transcendentals=queries * all_keys,
+        ),
+    )(block, bias, *parts)
+
+
+def tile_mixed(cells):
+    return lax.all_to_all(cells, "tile", split_axis=0, concat_axis=0, tiled=True)
+
+
+def by_heads(img_qkv, txt_kv, text_limit, tile_cols):
+    rows, grid_cols = img_qkv.shape[1:3]
+    heads = img_qkv.shape[4] // HD
+    text_rows = txt_kv.shape[1]
+    tiles = lax.axis_size("tile")
+    halves = grid_cols // tile_cols
+    own = rows * tile_cols
+    full = own * halves
+    text_half = text_rows // halves
+    me = lax.axis_index("col")
+
+    img = jnp.transpose(
+        img_qkv[0].reshape(rows, halves, tile_cols, 3, heads, HD), (4, 3, 1, 0, 2, 5)
+    ).reshape(heads, 3, halves, own, HD)
+    txt = jnp.transpose(txt_kv[0].reshape(text_rows, 2, heads, HD), (2, 1, 0, 3))
+
+    img_a = img[:tiles].reshape(tiles, 3, full, HD)
+    txt_a = txt[:tiles]
+    send_a = jnp.concatenate(
+        [img_a[:, 0], img_a[:, 1], txt_a[:, 0], img_a[:, 2], txt_a[:, 1]], axis=1
+    )
+    got_a = tile_mixed(send_a)
+
+    img_b = img[tiles:]
+    txt_b = txt[tiles:].reshape(heads - tiles, 2, halves, text_half, HD)
+    send_b = jnp.stack(
+        [
+            jnp.concatenate(
+                [
+                    img_b[:, 0, half],
+                    img_b[:, 1, half],
+                    txt_b[:, 0, half],
+                    img_b[:, 2, half],
+                    txt_b[:, 1, half],
+                ],
+                axis=1,
+            )
+            for half in range(halves)
+        ]
+    )
+    mixed_b = lax.all_to_all(send_b, "col", split_axis=0, concat_axis=0, tiled=True)
+    got_b = tile_mixed(mixed_b.reshape(tiles, send_b.shape[2], HD))
+    other_b = lax.ppermute(got_b[:, own:], "col", [(0, 1), (1, 0)])
+
+    text_all = tiles * text_rows
+    image_all = tiles * full
+    place = jnp.arange(text_all, dtype=jnp.int32)
+    bias_a = jnp.where(place < text_limit, 0.0, -1e30).astype(jnp.float32)[None]
+    side, within = place // (tiles * text_half), place % (tiles * text_half)
+    place_b = (
+        within // text_half * text_rows
+        + jnp.where(side == 0, me, 1 - me) * text_half
+        + within % text_half
+    )
+    bias_b = jnp.where(place_b < text_limit, 0.0, -1e30).astype(jnp.float32)[None]
+
+    moves_a, moves_b = [], []
+    for t in range(tiles):
+        key, value = full, 2 * full + text_rows
+        moves_a.append((0, t, key, value, full, t * full))
+        moves_a.append((0, t, key + full, value + full, text_rows, image_all + t * text_rows))
+    for s in range(halves):
+        for t in range(tiles):
+            key = own if s == 0 else 0
+            value = key + own + text_half
+            slot = s * tiles + t
+            moves_b.append((s, t, key, value, own, slot * own))
+            moves_b.append(
+                (s, t, key + own, value + own, text_half, image_all + slot * text_half)
+            )
+    out_a = tile_mixed(attend(got_a, (), bias_a, full, tuple(moves_a), image_all, 512, 1024))
+    out_b = tile_mixed(
+        attend(got_b, (other_b,), bias_b, own, tuple(moves_b), image_all, 512, 1024)
+    )
+    out_a = jnp.transpose(out_a.reshape(tiles, halves, own, HD), (1, 0, 2, 3))
+    out_a = lax.all_to_all(out_a, "col", split_axis=0, concat_axis=0, tiled=True)
+    every = jnp.concatenate([out_a.reshape(halves * tiles, own, HD), out_b], axis=0)
+    order = [c * heads + t for c in range(halves) for t in range(tiles)]
+    order += [c * heads + h for c in range(halves) for h in range(tiles, heads)]
+    return every, order
 
 
 def body(
@@ -93,22 +253,28 @@
     own_rows = tile_rows * tile_cols
     text_limit = text_len[0]
     all_heads = local_heads * col_count
-    img_block = img_qkv[0].reshape(tile_rows, grid_cols, 3, local_heads, HD)
-    txt_block = txt_kv[0].reshape(1, text_rows, 2, local_heads, HD)
-    img_mixed, txt_mixed = (
-        lax.all_to_all(img_block, "col", split_axis=1, concat_axis=3, tiled=True),
-        lax.all_to_all(txt_block, "col", split_axis=1, concat_axis=3, tiled=True),
-    )
-    img_flat = img_mixed.reshape(own_rows, 3, all_heads, HD)
-    txt_flat = txt_mixed.reshape(text_rows // col_count, 2, all_heads, HD)
-    key_value = jnp.concatenate([img_flat[:, 1:], txt_flat], axis=0)
-    fold_step = make_fold(img_flat[:, 0], own_rows, text_rows // col_count, text_limit)
-    carry = fold_step(
-        start_carry(own_rows, all_heads),
-        lax.all_gather(key_value, ("tile", "col"), axis=0, tiled=True),
-        jnp.int32(0),
-    )
-    attended = finish(carry).reshape(own_rows, all_heads * HD)
+    tiles = lax.axis_size("tile")
+    if col_count == 2 and (local_heads - tiles) * col_count == tiles:
+        every, order = by_heads(img_qkv, txt_kv, text_limit, tile_cols)
+        attended = jnp.transpose(every, (1, 0, 2)).reshape(own_rows, all_heads * HD)
+        w_attn_out = jnp.concatenate([w_attn_out[h * HD : (h + 1) * HD] for h in order], axis=0)
+    else:
+        img_block = img_qkv[0].reshape(tile_rows, grid_cols, 3, local_heads, HD)
+        txt_block = txt_kv[0].reshape(1, text_rows, 2, local_heads, HD)
+        img_mixed, txt_mixed = (
+            lax.all_to_all(img_block, "col", split_axis=1, concat_axis=3, tiled=True),
+            lax.all_to_all(txt_block, "col", split_axis=1, concat_axis=3, tiled=True),
+        )
+        img_flat = img_mixed.reshape(own_rows, 3, all_heads, HD)
+        txt_flat = txt_mixed.reshape(text_rows // col_count, 2, all_heads, HD)
+        key_value = jnp.concatenate([img_flat[:, 1:], txt_flat], axis=0)
+        fold_step = make_fold(img_flat[:, 0], own_rows, text_rows // col_count, text_limit)
+        carry = fold_step(
+            start_carry(own_rows, all_heads),
+            lax.all_gather(key_value, ("tile", "col"), axis=0, tiled=True),
+            jnp.int32(0),
+        )
+        attended = finish(carry).reshape(own_rows, all_heads * HD)
     branch = jnp.dot(attended, w_attn_out, preferred_element_type=jnp.float32)
     step_now = step_index[0]
     mod_now = lax.dynamic_index_in_dim(modulation, step_now, 0, keepdims=False)[0]

time: 457 us -> 268 us (0.59)
  waiting for transfers between devices: 251 us -> 118 us
  matrix products: 101 us -> 13.9 us
  Pallas kernels: 0 us -> 41.6 us
  other arithmetic: 39.1 us -> 3.95 us
  local copies, waits for them, and re-layouts: 33.4 us -> 51.2 us
  between operations: 17 us -> 3.58 us
  blocking collectives: 0 us -> 10.5 us
  starting transfers between devices: 15.3 us -> 24.3 us
    all_gather x1 -> x0, waiting for transfers between devices: 244 us -> none  [body(): lax.all_gather(key_value, ('tile', 'col'), axis=0, tiled=True)]
    all_to_all x2 -> x4, waiting for transfers between devices: 3.28 us -> 114 us  [tile_mixed(): lax.all_to_all(cells, 'tile', split_axis=0, concat_axis=0, tiled=True)]
    dot_general x2 -> x0, matrix products: 86.2 us -> none  [the longest x1 43.7 us: fold_step(): jnp.einsum('qhd,khd->hqk', queries, piece[:, 0], preferred_element_type=j...]
    pallas_call x0 -> x2, Pallas kernels: none -> 41.6 us  [attend(): pl.pallas_call(functools.partial(attend_kernel, moves, key_chunk, image_k...]
    reduce_sum x1 -> x0, other arithmetic: 35.4 us -> none  [fold_step(): run_sum = jnp.sum(weights, axis=2)]
    slice x1 -> x9, local copies, waits for them, and re-layouts: 0.3 us -> 21.9 us  [the longest x2 9.75 us: body(): w_attn_out[h * HD:(h + 1) * HD]]
    all_to_all x0 -> x2, blocking collectives: none -> 10.5 us  [the longest x1 5.97 us: by_heads(): lax.all_to_all(send_b, 'col', split_axis=0, concat_axis=0, tiled=True)]
    another operation x3 -> x2, local copies, waits for them, and re-layouts: 22.4 us -> 12.8 us  [the longest x1 10.8 us: by_heads(): img_qkv[0].reshape(rows, halves, tile_cols, 3, heads, HD)]
  transfers between devices with their start and end apart: 7 -> 9, of which waited for: 4 -> 6; matrix products, arithmetic and copies ran while one was open for 2% -> 10% of each run, Pallas kernels for 0% -> 16%
where the time goes in v1:
time: 268 us; the launch traced here: 267 us
  waiting for transfers between devices  118 us (44%)
  local copies, waits for them, and re-layouts  51.2 us (19%)
  Pallas kernels  41.6 us (16%)
  starting transfers between devices  24.3 us (9%)
  matrix products  13.9 us (5%)
  blocking collectives  10.5 us (4%)
  other arithmetic  3.95 us (1%)
  between operations  3.58 us (1%)
    all_to_all x4, waiting for transfers between devices, tile_mixed(): lax.all_to_all(cells, 'tile', split_axis=0, concat_axis=0, tiled=True)  114 us
    pallas_call x2, Pallas kernels, attend(): pl.pallas_call(functools.partial(attend_kernel, moves, key_chunk, image_k...  41.6 us
    all_to_all x4, starting transfers between devices, tile_mixed(): lax.all_to_all(cells, 'tile', split_axis=0, concat_axis=0, tiled=True)  18.9 us
    another operation x1, local copies, waits for them, and re-layouts, by_heads(): img_qkv[0].reshape(rows, halves, tile_cols, 3, heads, HD)  10.8 us
    unnamed x26, local copies, waits for them, and re-layouts  10.1 us
    slice x2, local copies, waits for them, and re-layouts, body(): w_attn_out[h * HD:(h + 1) * HD]  9.75 us
    dot_general x1, matrix products, body(): branch = jnp.dot(attended, w_attn_out, preferred_element_type=jnp.float32)  8.68 us
    all_to_all x1, blocking collectives, by_heads(): lax.all_to_all(send_b, 'col', split_axis=0, concat_axis=0, tiled=True)  5.97 us
  transfers between devices with their start and end apart: 9, of which 6 were waited for; matrix products, arithmetic and copies ran while one was open for 10% of the time, Pallas kernels for 16%

profile of v1, /device:TPU:0, one launch (start us, length us, event | category | flops | bytes accessed | tf_op | source)
XLA Modules:
  0.0 267.1 jit_solution(10963778902511745880)
XLA Ops:
  0.6 10.8 %reshape_squeeze.10 = bf16[16,2,32,3,6,128]{5,4,2,1,3,0:T(8,128)(2,1)} reshape(bf16[1,16,64,3,768]{4,2,3,1,0:T(8,128)(2,1)} %param.11) | data formatting | bytes 9437184 | tf_op jit(solution)/shard_map/reshape;squeeze | solution.py:164
  11.5 4.5 %slice.233 = bf16[2,3,2,16,32,128]{5,0,4,2,1,3:T(2,128)(2,1)S(1)} slice(bf16[6,3,2,16,32,128]{5,0,4,2,1,3:T(8,128)(2,1)} %bitcast.169), slice={[4:6], [0:3], [0:2], [0:16], [0:32], [0:128]} | slice | bytes 3145728 | tf_op jit(solution)/shard_map/slice | solution.py:175
  16.6 0.7 fusion.44
  17.3 0.9 fusion.43
  18.2 1.9 copy.49
  20.1 2.0 copy.50
  22.1 0.9 slice.236
  23.6 0.9 fusion.42
  24.5 0.6 fusion.49
  25.2 0.7 fusion.39
  26.5 1.6 pad_maximum_fusion
  28.1 6.0 %all_to_all.30 = bf16[2,2,1664,128]{3,2,1,0:T(8,128)(2,1)} all-to-all(bf16[2,2,1664,128]{3,2,1,0:T(8,128)(2,1)S(1)} %pad_maximum_fusion), channel_id=1, replica_groups=mesh['req'=4,'tile'=4,'col'=2] {'col'}, dimensions={0} | all-to-all | bytes 3407872 | tf_op jit(solution)/shard_map/all_to_all | solution.py:192
  34.0 6.3 %all-to-all-start.4 = ((bf16[4,1664,128]{2,1,0:T(8,128)(2,1)}), bf16[4,1664,128]{2,1,0:T(8,128)(2,1)S(1)}, u32[]{:S(2)}, u32[]{:S(2)}) async-start(bf16[4,1664,128]{2,1,0:T(8,128)(2,1)} %bitcast.180), calls=%async_computation.4 | async-start | bytes 3407872 | tf_op jit(solution)/shard_map/all_to_all | solution.py:149
  40.3 4.3 %slice.227 = bf16[4,3,2,16,32,128]{5,0,4,2,1,3:T(4,128)(2,1)S(1)} slice(bf16[6,3,2,16,32,128]{5,0,4,2,1,3:T(8,128)(2,1)} %bitcast.170), slice={[0:4], [0:3], [0:2], [0:16], [0:32], [0:128]} | slice | bytes 6291456 | tf_op jit(solution)/shard_map/slice | solution.py:168
  44.6 0.7 copy.48
  45.3 1.2 fusion.20
  46.5 1.2 fusion.19
  47.7 0.7 fusion.46
  48.4 1.2 fusion.18
  49.6 0.7 fusion.45
  50.3 30.1 %all-to-all-done.4.q_ref.refs_0_ = bf16[4,1664,128]{2,1,0:T(8,128)(2,1)S(1)} async-done(((bf16[4,1664,128]{2,1,0:T(8,128)(2,1)}), bf16[4,1664,128]{2,1,0:T(8,128)(2,1)S(1)}, u32[]{:S(2)}, u32[]{:S(2)}) %all-to-all-start.4) | async-done | bytes 1703968 | tf_op jit(solution)/shard_map/all_to_all | solution.py:149
  80.4 4.7 %all-to-all-start = ((bf16[4,3328,128]{2,1,0:T(8,128)(2,1)}), bf16[4,3328,128]{2,1,0:T(8,128)(2,1)}, u32[]{:S(2)}, u32[]{:S(2)}) async-start(bf16[4,3328,128]{2,1,0:T(8,128)(2,1)} %fusion.45), calls=%async_computation | async-start | bytes 6815744 | tf_op jit(solution)/shard_map/all_to_all | solution.py:149
  86.4 0.8 copy.64
  89.1 1.4 dynamic-slice_add_fusion
  90.5 1.1 slice.245
  91.6 69.4 %all-to-all-done.q_ref.refs_0_ = bf16[4,3328,128]{2,1,0:T(8,128)(2,1)} async-done(((bf16[4,3328,128]{2,1,0:T(8,128)(2,1)}), bf16[4,3328,128]{2,1,0:T(8,128)(2,1)}, u32[]{:S(2)}, u32[]{:S(2)}) %all-to-all-start) | async-done | bytes 3407904 | tf_op jit(solution)/shard_map/all_to_all | solution.py:149
  161.0 28.1 %shard_map.130 = bf16[4,1024,128]{2,1,0:T(8,128)(2,1)} custom-call(bf16[4,3328,128]{2,1,0:T(8,128)(2,1)} %all-to-all-done.q_ref.refs_0_, f32[1,512]{1,0:T(1,128)S(1)} %compare_select_fusion.2.bias_ref, bf16[4,3328,128]{2,1,0:T(8,128)(2,1)} %all-to-all-done.q_ref.refs_0_), custom_call_target="tpu_custom_call" | custom-call | flops 14495514624 | bytes 5505024 | tf_op jit(solution)/shard_map/pallas_call | solution.py:125
  189.1 4.4 %all-to-all-start.1 = ((bf16[4,1024,128]{2,1,0:T(8,128)(2,1)}), bf16[4,1024,128]{2,1,0:T(8,128)(2,1)}, u32[]{:S(2)}, u32[]{:S(2)}) async-start(bf16[4,1024,128]{2,1,0:T(8,128)(2,1)} %shard_map.130), calls=%async_computation.1 | async-start | bytes 2097152 | tf_op jit(solution)/shard_map/all_to_all | solution.py:149
  193.5 5.9 %fusion.76 = (bf16[512,3072]{1,0:T(8,128)(2,1)}, bf16[512,3072]{1,0:T(8,128)(2,1)}) fusion(bf16[1536,3072]{1,0:T(8,128)(2,1)} %param.16), kind=kLoop, calls=%fused_computation.122 | loop fusion | bytes 12582912 | tf_op jit(solution)/shard_map/slice | solution.py:260
  199.5 13.5 %shard_map.131 = bf16[4,512,128]{2,1,0:T(8,128)(2,1)} custom-call(bf16[4,1664,128]{2,1,0:T(8,128)(2,1)S(1)} %all-to-all-done.4.q_ref.refs_0_, f32[1,512]{1,0:T(1,128)S(1)} %compare_select_fusion.bias_ref, bf16[4,1664,128]{2,1,0:T(8,128)(2,1)S(1)} %all-to-all-done.4.q_ref.refs_0_, bf16[4,1152,128]{2,1,0:T(8,128)(2,1)S(1)} %collective-permute-done.refs_1_), custom_call_target="tpu_custom_call" | custom-call | flops 7247757312 | bytes 3932160 | tf_op jit(solution)/shard_map/pallas_call | solution.py:125
  213.0 5.7 %all-to-all-done.1 = bf16[4,1024,128]{2,1,0:T(8,128)(2,1)} async-done(((bf16[4,1024,128]{2,1,0:T(8,128)(2,1)}), bf16[4,1024,128]{2,1,0:T(8,128)(2,1)}, u32[]{:S(2)}, u32[]{:S(2)}) %all-to-all-start.1) | async-done | bytes 1048608 | tf_op jit(solution)/shard_map/all_to_all | solution.py:149
  218.6 3.5 %all-to-all-start.5 = ((bf16[4,512,128]{2,1,0:T(8,128)(2,1)}), bf16[4,512,128]{2,1,0:T(8,128)(2,1)S(1)}, u32[]{:S(2)}, u32[]{:S(2)}) async-start(bf16[4,512,128]{2,1,0:T(8,128)(2,1)} %shard_map.131), calls=%async_computation.5 | async-start | bytes 1048576 | tf_op jit(solution)/shard_map/all_to_all | solution.py:149
  222.1 3.8 %fusion.77 = (bf16[256,3072]{1,0:T(8,128)(2,1)}, bf16[256,3072]{1,0:T(8,128)(2,1)}) fusion(bf16[1536,3072]{1,0:T(8,128)(2,1)} %param.16), kind=kLoop, calls=%fused_computation.123 | loop fusion | bytes 6291456 | tf_op jit(solution)/shard_map/slice | solution.py:260
  225.9 1.3 copy.81
  227.2 8.8 %all-to-all-done.5 = bf16[4,512,128]{2,1,0:T(8,128)(2,1)S(1)} async-done(((bf16[4,512,128]{2,1,0:T(8,128)(2,1)}), bf16[4,512,128]{2,1,0:T(8,128)(2,1)S(1)}, u32[]{:S(2)}, u32[]{:S(2)}) %all-to-all-start.5) | async-done | bytes 524320 | tf_op jit(solution)/shard_map/all_to_all | solution.py:149
  236.1 4.6 %all_to_all.31 = bf16[2,4,512,128]{3,2,1,0:T(8,128)(2,1)S(1)} all-to-all(bf16[2,4,512,128]{3,2,1,0:T(8,128)(2,1)S(1)} %bitcast.185), channel_id=1, replica_groups=mesh['req'=4,'tile'=4,'col'=2] {'col'}, dimensions={0} | all-to-all | bytes 2097152 | tf_op jit(solution)/shard_map/all_to_all | solution.py:227
  240.8 0.7 copy.62
  241.5 8.7 %fusion.79 = (f32[512]{0:T(512)S(1)}, f32[512,3072]{1,0:T(8,128)S(1)}) fusion(bf16[512,1536]{0,1:T(8,128)(2,1)S(1)} %bitcast.187, bf16[256,3072]{1,0:T(8,128)(2,1)} %get-tuple-element.9, bf16[256,3072]{1,0:T(8,128)(2,1)} %get-tuple-element.8, bf16[512,3072]{1,0:T(8,128)(2,1)} %get-tuple-element.7, bf16[512,3072]{1,0:T(8,128)(2,1)} %get-tuple-element.6, ...), kind=kOutput, calls=%fused_computation.125 | convolution fusion | flops 4875877888 | bytes 20461568 | tf_op jit(solution)/shard_map/dot_general | solution.py:278
  250.2 0.8 multiply_reduce_fusion
  251.1 1.3 multiply_add_fusion
  252.6 1.3 collective-permute-start.1
  253.9 1.3 collective-permute-start.2
  255.6 0.8 copy.63
  256.8 2.9 %collective-permute-done.2 = f32[1,32,64]{1,2,0:T(8,128)S(1)} collective-permute-done((f32[1,32,64]{1,2,0:T(8,128)S(1)}, f32[1,32,64]{1,2,0:T(8,128)S(1)}, u32[]{:S(2)}, u32[]{:S(2)}) %collective-permute-start.2) | collective-permute-done | bytes 8224 | tf_op jit(solution)/shard_map/ppermute | solution.py:27
  259.8 1.3 collective-permute-start.3
  261.1 1.5 collective-permute-start.4
  263.0 1.2 collective-permute-done.4
  266.1 1.1 fusion.17
  (44 shorter events, 6.0 us)
Async XLA Ops:
  0.6 250.3 %copy-start = (bf16[3072,64]{0,1:T(8,128)(2,1)S(1)}, bf16[3072,64]{0,1:T(8,128)(2,1)}, u32[]{:S(2)}) copy-start(bf16[3072,64]{0,1:T(8,128)(2,1)} %param.17) | copy-start | bytes 1179652
  34.0 46.4 %all-to-all-start.4 = ((bf16[4,1664,128]{2,1,0:T(8,128)(2,1)}), bf16[4,1664,128]{2,1,0:T(8,128)(2,1)S(1)}, u32[]{:S(2)}, u32[]{:S(2)}) async-start(bf16[4,1664,128]{2,1,0:T(8,128)(2,1)} %bitcast.180), calls=%async_computation.4 | async-start | bytes 3407872 | tf_op jit(solution)/shard_map/all_to_all | solution.py:149
  45.3 2.4 copy-start.2
  50.2 36.2 %copy-start.4 = (f32[1,16,32,64]{3,2,1,0:T(8,128)S(1)}, f32[1,16,32,64]{3,2,1,0:T(8,128)}, u32[]{:S(2)}) copy-start(f32[1,16,32,64]{3,2,1,0:T(8,128)} %param.18) | copy-start | bytes 393220
  50.3 37.0 %copy-start.7 = (f32[29]{0:T(128)S(1)}, f32[29]{0:T(128)}, u32[]{:S(2)}) copy-start(f32[29]{0:T(128)} %param.19) | copy-start | bytes 352
  80.4 80.6 %all-to-all-start = ((bf16[4,3328,128]{2,1,0:T(8,128)(2,1)}), bf16[4,3328,128]{2,1,0:T(8,128)(2,1)}, u32[]{:S(2)}, u32[]{:S(2)}) async-start(bf16[4,3328,128]{2,1,0:T(8,128)(2,1)} %fusion.45), calls=%async_computation | async-start | bytes 6815744 | tf_op jit(solution)/shard_map/all_to_all | solution.py:149
  91.6 107.9 %collective-permute-start = (bf16[4,1152,128]{2,1,0:T(8,128)(2,1)}, bf16[4,1152,128]{2,1,0:T(8,128)(2,1)S(1)}, u32[]{:S(2)}, u32[]{:S(2)}) collective-permute-start(bf16[4,1152,128]{2,1,0:T(8,128)(2,1)} %slice.245), channel_id=1, source_target_pairs={{0,1},{1,0},{2,3},{3,2},{4,5},{5,4},{6,7},{7,6},{8,9},{9,8},{10,11... | collective-permute-start | bytes 3538952 | tf_op jit(solution)/shard_map/ppermute | solution.py:194
  189.1 29.5 %all-to-all-start.1 = ((bf16[4,1024,128]{2,1,0:T(8,128)(2,1)}), bf16[4,1024,128]{2,1,0:T(8,128)(2,1)}, u32[]{:S(2)}, u32[]{:S(2)}) async-start(bf16[4,1024,128]{2,1,0:T(8,128)(2,1)} %shard_map.130), calls=%async_computation.1 | async-start | bytes 2097152 | tf_op jit(solution)/shard_map/all_to_all | solution.py:149
  218.6 17.4 %all-to-all-start.5 = ((bf16[4,512,128]{2,1,0:T(8,128)(2,1)}), bf16[4,512,128]{2,1,0:T(8,128)(2,1)S(1)}, u32[]{:S(2)}, u32[]{:S(2)}) async-start(bf16[4,512,128]{2,1,0:T(8,128)(2,1)} %shard_map.131), calls=%async_computation.5 | async-start | bytes 1048576 | tf_op jit(solution)/shard_map/all_to_all | solution.py:149
  250.2 0.9 copy-start.5
  250.2 0.9 copy-start.6
  251.1 4.1 %copy-start.3 = (f32[3,3,64,64]{3,2,1,0:T(8,128)S(1)}, f32[3,3,64,64]{3,2,1,0:T(8,128)}, u32[]{:S(2)}) copy-start(f32[3,3,64,64]{3,2,1,0:T(8,128)} %param.21) | copy-start | bytes 442372
  252.5 13.6 %copy-start.1 = (f32[512,64]{1,0:T(8,128)}, f32[512,64]{1,0:T(8,128)S(1)}, u32[]{:S(2)}) copy-start(f32[512,64]{1,0:T(8,128)S(1)} %copy.65) | copy-start | bytes 393220
  252.6 3.8 %collective-permute-start.1 = (f32[1,32,64]{1,2,0:T(8,128)S(1)}, f32[1,32,64]{1,2,0:T(8,128)S(1)}, u32[]{:S(2)}, u32[]{:S(2)}) collective-permute-start(f32[1,32,64]{1,2,0:T(8,128)S(1)} %get-tuple-element.21), channel_id=1, source_target_pairs={{0,2},{2,4},{4,6},{1,3},{3,5},{5,7},{8,10},{10,12},{12,14},{9,11},... | collective-permute-start | bytes 24584 | tf_op jit(solution)/shard_map/ppermute | solution.py:25
  253.9 5.8 %collective-permute-start.2 = (f32[1,32,64]{1,2,0:T(8,128)S(1)}, f32[1,32,64]{1,2,0:T(8,128)S(1)}, u32[]{:S(2)}, u32[]{:S(2)}) collective-permute-start(f32[1,32,64]{1,2,0:T(8,128)S(1)} %get-tuple-element.22), channel_id=1, source_target_pairs={{2,0},{4,2},{6,4},{3,1},{5,3},{7,5},{10,8},{12,10},{14,12},{11,9},... | collective-permute-start | bytes 24584 | tf_op jit(solution)/shard_map/ppermute | solution.py:27
  259.8 3.2 %collective-permute-start.3 = (f32[18,1,64]{2,1,0:T(1,128)S(1)}, f32[18,1,64]{2,1,0:T(1,128)S(1)}, u32[]{:S(2)}, u32[]{:S(2)}) collective-permute-start(f32[18,1,64]{2,1,0:T(1,128)S(1)} %get-tuple-element.19), channel_id=1, source_target_pairs={{0,1},{2,3},{4,5},{6,7},{8,9},{10,11},{12,13},{14,15},{16,17},{18,... | collective-permute-start | bytes 13832 | tf_op jit(solution)/shard_map/ppermute | solution.py:25
  261.1 3.1 %collective-permute-start.4 = (f32[18,1,64]{2,1,0:T(1,128)S(1)}, f32[18,1,64]{2,1,0:T(1,128)S(1)}, u32[]{:S(2)}, u32[]{:S(2)}) collective-permute-start(f32[18,1,64]{2,1,0:T(1,128)S(1)} %get-tuple-element.20), channel_id=1, source_target_pairs={{1,0},{3,2},{5,4},{7,6},{9,8},{11,10},{13,12},{15,14},{17,16},{19,... | collective-permute-start | bytes 13832 | tf_op jit(solution)/shard_map/ppermute | solution.py:27

commit v2 on v1

--- a/solution.py
+++ b/solution.py
@@ -20,6 +20,13 @@
         ends = count - 1
         head = lax.slice_in_dim(cells, 0, width, axis=dim)
         tail = lax.slice_in_dim(cells, cells.shape[dim] - width, cells.shape[dim], axis=dim)
+        if count == 2:
+            me = lax.axis_index(axis)
+            came = lax.ppermute(jnp.where(me == 0, tail, head), axis, [(0, 1), (1, 0)])
+            cells = jnp.concatenate(
+                [jnp.where(me == 0, 0.0, came), cells, jnp.where(me == 0, came, 0.0)], axis=dim
+            )
+            continue
         cells = jnp.concatenate(
             [
                 lax.ppermute(tail, axis, [(i, (i + 1) % count) for i in range(ends)]),
@@ -145,8 +152,104 @@
     )(block, bias, *parts)
 
 
+def pack_whole_kernel(rows, halves, tile_cols, img_ref, txt_ref, o_ref):
+    text_rows = txt_ref.shape[1]
+    at = 0
+    for part in range(3):
+        for half in range(halves):
+            for row in range(rows):
+                start = (row * halves + half) * tile_cols
+                o_ref[0, at : at + tile_cols, :] = img_ref[part, start : start + tile_cols, :]
+                at += tile_cols
+        if part:
+            o_ref[0, at : at + text_rows, :] = txt_ref[part - 1]
+            at += text_rows
+
+
+def pack_halves_kernel(rows, halves, tile_cols, img_ref, txt_ref, o_ref):
+    text_half = txt_ref.shape[1] // halves
+    for half in range(halves):
+        at = 0
+        for part in range(3):
+            for row in range(rows):
+                start = (row * halves + half) * tile_cols
+                o_ref[half, 0, at : at + tile_cols, :] = img_ref[
+                    part, start : start + tile_cols, :
+                ]
+                at += tile_cols
+            if part:
+                o_ref[half, 0, at : at + text_half, :] = txt_ref[
+                    part - 1, half * text_half : (half + 1) * text_half, :
+                ]
+                at += text_half
+
+
+def pack_whole(img, txt, count, rows, halves, tile_cols):
+    tokens, text_rows = img.shape[1], txt.shape[1]
+    length = 3 * tokens + 2 * text_rows
+    return pl.pallas_call(
+        functools.partial(pack_whole_kernel, rows, halves, tile_cols),
+        grid=(count,),
+        out_shape=jax.ShapeDtypeStruct((count, length, HD), img.dtype),
+        in_specs=[
+            pl.BlockSpec((3, tokens, HD), lambda i: (0, 0, i)),
+            pl.BlockSpec((2, text_rows, HD), lambda i: (0, 0, i)),
+        ],
+        out_specs=pl.BlockSpec((1, length, HD), lambda i: (i, 0, 0)),
+        compiler_params=pltpu.CompilerParams(vmem_limit_bytes=32 * 1024 * 1024),
+        cost_estimate=pl.CostEstimate(
+            flops=0, bytes_accessed=4 * count * length * HD, transcendentals=0
+        ),
+    )(img, txt)
+
+
+def pack_halves(img, txt, first, count, rows, halves, tile_cols):
+    tokens, text_rows = img.shape[1], txt.shape[1]
+    length = (3 * tokens + 2 * text_rows) // halves
+    return pl.pallas_call(
+        functools.partial(pack_halves_kernel, rows, halves, tile_cols),
+        grid=(count,),
+        out_shape=jax.ShapeDtypeStruct((halves, count, length, HD), img.dtype),
+        in_specs=[
+            pl.BlockSpec((3, tokens, HD), lambda i: (0, 0, first + i)),
+            pl.BlockSpec((2, text_rows, HD), lambda i: (0, 0, first + i)),
+        ],
+        out_specs=pl.BlockSpec((halves, 1, length, HD), lambda i: (0, i, 0, 0)),
+        compiler_params=pltpu.CompilerParams(vmem_limit_bytes=32 * 1024 * 1024),
+        cost_estimate=pl.CostEstimate(
+            flops=0, bytes_accessed=4 * halves * count * length * HD, transcendentals=0
+        ),
+    )(img, txt)
+
+
 def tile_mixed(cells):
     return lax.all_to_all(cells, "tile", split_axis=0, concat_axis=0, tiled=True)
+
+
+def tile_stepped(cells):
+    count = lax.axis_size("tile")
+    me = lax.axis_index("tile")
+    held = []
+    for step in range(count):
+        block = lax.dynamic_index_in_dim(cells, (me + step) % count, 0, keepdims=True)
+        if step:
+            block = lax.ppermute(block, "tile", [(i, (i + step) % count) for i in range(count)])
+        held.append(block)
+    held = jnp.concatenate(held, axis=0)
+    return jnp.concatenate(
+        [
+            lax.dynamic_index_in_dim(held, (me - source + count) % count, 0, keepdims=True)
+            for source in range(count)
+        ],
+        axis=0,
+    )
+
+
+def col_swapped(cells, me, dim):
+    kept = lax.dynamic_index_in_dim(cells, me, dim, keepdims=False)
+    sent = lax.dynamic_index_in_dim(cells, 1 - me, dim, keepdims=False)
+    came = lax.ppermute(sent, "col", [(0, 1), (1, 0)])
+    return [jnp.where(me == 0, kept, came), jnp.where(me == 0, came, kept)]
 
 
 def by_heads(img_qkv, txt_kv, text_limit, tile_cols):
@@ -160,38 +263,15 @@
     text_half = text_rows // halves
     me = lax.axis_index("col")
 
-    img = jnp.transpose(
-        img_qkv[0].reshape(rows, halves, tile_cols, 3, heads, HD), (4, 3, 1, 0, 2, 5)
-    ).reshape(heads, 3, halves, own, HD)
-    txt = jnp.transpose(txt_kv[0].reshape(text_rows, 2, heads, HD), (2, 1, 0, 3))
-
-    img_a = img[:tiles].reshape(tiles, 3, full, HD)
-    txt_a = txt[:tiles]
-    send_a = jnp.concatenate(
-        [img_a[:, 0], img_a[:, 1], txt_a[:, 0], img_a[:, 2], txt_a[:, 1]], axis=1
-    )
+    img = jnp.transpose(img_qkv[0].reshape(full, 3, heads * HD), (1, 0, 2))
+    txt = jnp.transpose(txt_kv[0], (1, 0, 2))
+    send_a = pack_whole(img, txt, tiles, rows, halves, tile_cols)
+    send_a, img, txt = lax.optimization_barrier((send_a, img, txt))
     got_a = tile_mixed(send_a)
-
-    img_b = img[tiles:]
-    txt_b = txt[tiles:].reshape(heads - tiles, 2, halves, text_half, HD)
-    send_b = jnp.stack(
-        [
-            jnp.concatenate(
-                [
-                    img_b[:, 0, half],
-                    img_b[:, 1, half],
-                    txt_b[:, 0, half],
-                    img_b[:, 2, half],
-                    txt_b[:, 1, half],
-                ],
-                axis=1,
-            )
-            for half in range(halves)
-        ]
-    )
-    mixed_b = lax.all_to_all(send_b, "col", split_axis=0, concat_axis=0, tiled=True)
-    got_b = tile_mixed(mixed_b.reshape(tiles, send_b.shape[2], HD))
-    other_b = lax.ppermute(got_b[:, own:], "col", [(0, 1), (1, 0)])
+    send_b = pack_halves(img, txt, tiles, heads - tiles, rows, halves, tile_cols)
+    mixed_b = jnp.concatenate(col_swapped(send_b, me, 0), axis=0)
+    mixed_b, got_a = lax.optimization_barrier((mixed_b, got_a))
+    got_b = tile_mixed(mixed_b)
 
     text_all = tiles * text_rows
     image_all = tiles * full
@@ -219,16 +299,17 @@
             moves_b.append(
                 (s, t, key + own, value + own, text_half, image_all + slot * text_half)
             )
-    out_a = tile_mixed(attend(got_a, (), bias_a, full, tuple(moves_a), image_all, 512, 1024))
-    out_b = tile_mixed(
-        attend(got_b, (other_b,), bias_b, own, tuple(moves_b), image_all, 512, 1024)
-    )
-    out_a = jnp.transpose(out_a.reshape(tiles, halves, own, HD), (1, 0, 2, 3))
-    out_a = lax.all_to_all(out_a, "col", split_axis=0, concat_axis=0, tiled=True)
-    every = jnp.concatenate([out_a.reshape(halves * tiles, own, HD), out_b], axis=0)
-    order = [c * heads + t for c in range(halves) for t in range(tiles)]
-    order += [c * heads + h for c in range(halves) for h in range(tiles, heads)]
-    return every, order
+    raw_a = attend(got_a, (), bias_a, full, tuple(moves_a), image_all, 512, 1024)
+    raw_a, got_b = lax.optimization_barrier((raw_a, got_b))
+    out_a = tile_mixed(raw_a)
+    other_b = lax.ppermute(got_b[:, own:], "col", [(0, 1), (1, 0)])
+    raw_b = attend(got_b, (other_b,), bias_b, own, tuple(moves_b), image_all, 512, 1024)
+    out_b = tile_stepped(raw_b)
+    out_a, raw_b = lax.optimization_barrier((out_a, raw_b))
+    low, high = col_swapped(out_a.reshape(tiles, halves, own, HD), me, 1)
+    third = heads - tiles
+    every = jnp.concatenate([low, out_b[:third], high, out_b[third:]], axis=0)
+    return jnp.transpose(every, (1, 0, 2)).reshape(own, halves * heads * HD)
 
 
 def body(
@@ -255,9 +336,7 @@
     all_heads = local_heads * col_count
     tiles = lax.axis_size("tile")
     if col_count == 2 and (local_heads - tiles) * col_count == tiles:
-        every, order = by_heads(img_qkv, txt_kv, text_limit, tile_cols)
-        attended = jnp.transpose(every, (1, 0, 2)).reshape(own_rows, all_heads * HD)
-        w_attn_out = jnp.concatenate([w_attn_out[h * HD : (h + 1) * HD] for h in order], axis=0)
+        attended = by_heads(img_qkv, txt_kv, text_limit, tile_cols)
     else:
         img_block = img_qkv[0].reshape(tile_rows, grid_cols, 3, local_heads, HD)
         txt_block = txt_kv[0].reshape(1, text_rows, 2, local_heads, HD)
@@ -294,7 +373,7 @@
     sigma_step = sigmas[step_now + 1] - sigmas[step_now]
     updated = latent[0].reshape(own_rows, channels) + sigma_step * velocity
     grid_field = updated.reshape(tile_rows, tile_cols, channels)
-    padded = padded_2(grid_field, (("tile", 0), ("col", 1)), 1)
+    padded = padded_2(grid_field, (("col", 1), ("tile", 0)), 1)
     preview = jnp.zeros((tile_rows, tile_cols, channels), jnp.float32)
     for row_off in range(3):
         for col_off in range(3):

time: 268 us -> 205 us (0.76)
  local copies, waits for them, and re-layouts: 51.2 us -> 16.6 us
  waiting for transfers between devices: 118 us -> 97.7 us
  blocking collectives: 10.5 us -> 0 us
    all_to_all x4 -> x3, waiting for transfers between devices: 114 us -> 91.2 us  [tile_mixed(): lax.all_to_all(cells, 'tile', split_axis=0, concat_axis=0, tiled=True)]
    slice x9 -> x0, local copies, waits for them, and re-layouts: 20.8 us -> none  [the longest x2 9.75 us: body(): w_attn_out[h * HD:(h + 1) * HD]]
    another operation x2 -> x0, local copies, waits for them, and re-layouts: 12.8 us -> none  [the longest x1 10.8 us: by_heads(): img_qkv[0].reshape(rows, halves, tile_cols, 3, heads, HD)]
    all_to_all x2 -> x0, blocking collectives: 10.5 us -> none  [the longest x1 5.97 us: by_heads(): lax.all_to_all(send_b, 'col', split_axis=0, concat_axis=0, tiled=True)]
    ppermute x0 -> x6, starting transfers between devices: none -> 6.45 us  [the longest x3 5.76 us: tile_stepped(): lax.ppermute(block, 'tile', [(i, (i + step) % count) for i in range(count)])]
    all_to_all x4 -> x3, starting transfers between devices: 18.9 us -> 14.1 us  [tile_mixed(): lax.all_to_all(cells, 'tile', split_axis=0, concat_axis=0, tiled=True)]
    dynamic_slice x0 -> x9, local copies, waits for them, and re-layouts: none -> 2.91 us  [the longest x2 1.5 us: col_swapped(): kept = lax.dynamic_index_in_dim(cells, me, dim, keepdims=False)]
    unnamed x26 -> x29, local copies, waits for them, and re-layouts: 10.1 us -> 10.8 us
  transfers between devices with their start and end apart: 9 -> 12, of which waited for: 6 -> 5; matrix products, arithmetic and copies ran while one was open for 10% -> 5% of each run, Pallas kernels for 16% -> 20%
where the time goes in v2:
time: 205 us; the launch traced here: 204 us
  waiting for transfers between devices  97.7 us (48%)
  Pallas kernels  42.5 us (21%)
  starting transfers between devices  24.2 us (12%)
  local copies, waits for them, and re-layouts  16.6 us (8%)
  matrix products  13.6 us (7%)
  other arithmetic  6.16 us (3%)
  between operations  3.75 us (2%)
    all_to_all x3, waiting for transfers between devices, tile_mixed(): lax.all_to_all(cells, 'tile', split_axis=0, concat_axis=0, tiled=True)  91.2 us
    pallas_call x2, Pallas kernels, attend(): pl.pallas_call(functools.partial(attend_kernel, moves, key_chunk, image_k...  40.9 us
    all_to_all x3, starting transfers between devices, tile_mixed(): lax.all_to_all(cells, 'tile', split_axis=0, concat_axis=0, tiled=True)  14.1 us
    unnamed x29, local copies, waits for them, and re-layouts  10.8 us
    dot_general x1, matrix products, body(): branch = jnp.dot(attended, w_attn_out, preferred_element_type=jnp.float32)  8.26 us
    ppermute x3, starting transfers between devices, tile_stepped(): lax.ppermute(block, 'tile', [(i, (i + step) % count) for i in range(count)])  5.76 us
  transfers between devices with their start and end apart: 12, of which 5 were waited for; matrix products, arithmetic and copies ran while one was open for 5% of the time, Pallas kernels for 20%

profile of v2, /device:TPU:0, one launch (start us, length us, event | category | flops | bytes accessed | tf_op | source)
XLA Modules:
  0.0 204.4 jit_solution(14852266877764964000)
XLA Ops:
  0.7 2.9 %copy.25 = bf16[1,16,64,3,768]{4,2,1,3,0:T(8,128)(2,1)S(1)} copy(bf16[1,16,64,3,768]{4,2,3,1,0:T(8,128)(2,1)} %param.11) | data formatting | bytes 9437184 | tf_op args[0]
  3.6 0.9 shard_map.130
  4.6 2.1 %copy-done.1 = bf16[1,16,64,3,768]{4,2,1,3,0:T(8,128)(2,1)} copy-done((bf16[1,16,64,3,768]{4,2,1,3,0:T(8,128)(2,1)}, bf16[1,16,64,3,768]{4,2,1,3,0:T(8,128)(2,1)S(1)}, u32[]{:S(2)}) %copy-start.1) | copy-done | bytes 4718616
  6.7 1.8 copy-done.3
  8.5 6.3 %all-to-all-start = ((bf16[4,3328,128]{2,1,0:T(8,128)(2,1)}), bf16[4,3328,128]{2,1,0:T(8,128)(2,1)}, u32[]{:S(2)}, u32[]{:S(2)}) async-start(bf16[4,3328,128]{2,1,0:T(8,128)(2,1)} %copy-done.3), calls=%async_computation | async-start | bytes 6815744 | tf_op jit(solution)/shard_map/all_to_all | solution.py:226
  14.8 2.3 %copy-done.2 = bf16[1,16,64,3,768]{4,2,1,3,0:T(8,128)(2,1)S(1)} copy-done((bf16[1,16,64,3,768]{4,2,1,3,0:T(8,128)(2,1)S(1)}, bf16[1,16,64,3,768]{4,2,1,3,0:T(8,128)(2,1)}, u32[]{:S(2)}) %copy-start.2) | copy-done | bytes 4718616
  17.1 0.6 shard_map.131
  17.9 2.5 %collective-permute-done = bf16[2,1664,128]{2,1,0:T(8,128)(2,1)} collective-permute-done((bf16[2,1664,128]{2,1,0:T(8,128)(2,1)S(1)}, bf16[2,1664,128]{2,1,0:T(8,128)(2,1)}, u32[]{:S(2)}, u32[]{:S(2)}) %collective-permute-start) | collective-permute-done | bytes 852000 | tf_op jit(solution)/shard_map/ppermute | solution.py:251
  20.4 1.3 bitcast_select_fusion.1
  21.7 1.4 pad_maximum_fusion
  23.0 68.2 %all-to-all-done.q_ref.refs_0_ = bf16[4,3328,128]{2,1,0:T(8,128)(2,1)} async-done(((bf16[4,3328,128]{2,1,0:T(8,128)(2,1)}), bf16[4,3328,128]{2,1,0:T(8,128)(2,1)}, u32[]{:S(2)}, u32[]{:S(2)}) %all-to-all-start) | async-done | bytes 3407904 | tf_op jit(solution)/shard_map/all_to_all | solution.py:226
  91.2 3.6 %all-to-all-start.1 = ((bf16[4,1664,128]{2,1,0:T(8,128)(2,1)}), bf16[4,1664,128]{2,1,0:T(8,128)(2,1)S(1)}, u32[]{:S(2)}, u32[]{:S(2)}) async-start(bf16[4,1664,128]{2,1,0:T(8,128)(2,1)} %pad_maximum_fusion), calls=%async_computation.1 | async-start | bytes 3407872 | tf_op jit(solution)/shard_map/all_to_all | solution.py:226
  95.5 28.1 %shard_map.132 = bf16[4,1024,128]{2,1,0:T(8,128)(2,1)} custom-call(bf16[4,3328,128]{2,1,0:T(8,128)(2,1)} %all-to-all-done.q_ref.refs_0_, f32[1,512]{1,0:T(1,128)S(1)} %compare_select_fusion.2.bias_ref, bf16[4,3328,128]{2,1,0:T(8,128)(2,1)} %all-to-all-done.q_ref.refs_0_), custom_call_target="tpu_custom_call" | custom-call | flops 14495514624 | bytes 5505024 | tf_op jit(solution)/shard_map/pallas_call | solution.py:132
  123.6 10.3 %all-to-all-done.1.q_ref.refs_0_ = bf16[4,1664,128]{2,1,0:T(8,128)(2,1)S(1)} async-done(((bf16[4,1664,128]{2,1,0:T(8,128)(2,1)}), bf16[4,1664,128]{2,1,0:T(8,128)(2,1)S(1)}, u32[]{:S(2)}, u32[]{:S(2)}) %all-to-all-start.1) | async-done | bytes 1703968 | tf_op jit(solution)/shard_map/all_to_all | solution.py:226
  133.9 1.1 slice.91
  135.0 4.3 %all-to-all-start.2 = ((bf16[4,1024,128]{2,1,0:T(8,128)(2,1)}), bf16[4,1024,128]{2,1,0:T(8,128)(2,1)}, u32[]{:S(2)}, u32[]{:S(2)}) async-start(bf16[4,1024,128]{2,1,0:T(8,128)(2,1)} %shard_map.132), calls=%async_computation.2 | async-start | bytes 2097152 | tf_op jit(solution)/shard_map/all_to_all | solution.py:226
  140.0 12.8 %shard_map.133 = bf16[4,512,128]{2,1,0:T(8,128)(2,1)S(1)} custom-call(bf16[4,1664,128]{2,1,0:T(8,128)(2,1)S(1)} %all-to-all-done.1.q_ref.refs_0_, f32[1,512]{1,0:T(1,128)S(1)} %compare_select_fusion.bias_ref, bf16[4,1664,128]{2,1,0:T(8,128)(2,1)S(1)} %all-to-all-done.1.q_ref.refs_0_, bf16[4,1152,128]{2,1,0:T(8,128)(2,1)S(1)} %collective-permute-done.1.refs_1_), custom_call_target="tpu_custom_call" | custom-call | flops 7247757312 | bytes 3932160 | tf_op jit(solution)/shard_map/pallas_call | solution.py:132
  152.8 0.7 constant_dynamic-slice_fusion.8
  153.5 1.9 collective-permute-start.3
  155.5 2.4 %collective-permute-start.4 = (bf16[1,512,128]{2,1,0:T(8,128)(2,1)S(1)}, bf16[1,512,128]{2,1,0:T(8,128)(2,1)S(1)}, u32[]{:S(2)}, u32[]{:S(2)}) collective-permute-start(bf16[1,512,128]{2,1,0:T(8,128)(2,1)S(1)} %get-tuple-element.35), channel_id=1, source_target_pairs={{0,4},{2,6},{4,0},{6,2},{1,5},{3,7},{5,1},{7,3},{8,12},{10,14},{12... | collective-permute-start | bytes 393224 | tf_op jit(solution)/shard_map/ppermute | solution.py:236
  157.8 1.5 collective-permute-start.5
  159.3 12.7 %all-to-all-done.2 = bf16[4,1024,128]{2,1,0:T(8,128)(2,1)} async-done(((bf16[4,1024,128]{2,1,0:T(8,128)(2,1)}), bf16[4,1024,128]{2,1,0:T(8,128)(2,1)}, u32[]{:S(2)}, u32[]{:S(2)}) %all-to-all-start.2) | async-done | bytes 1048608 | tf_op jit(solution)/shard_map/all_to_all | solution.py:226
  172.0 1.3 constant_dynamic-slice_fusion.10
  173.3 0.2 copy.28
  173.6 1.4 dynamic-slice_add_fusion
  175.1 0.6 fusion.48
  177.0 1.0 pad_maximum_fusion.1
  178.5 0.2 copy.27
  178.8 0.1 fusion.8
  178.9 0.1 fusion.9
  179.1 1.5 copy-done.11
  180.6 8.3 %fusion.49 = (f32[512]{0:T(512)S(1)}, f32[512,3072]{1,0:T(8,128)S(1)}) fusion(bf16[512,1536]{0,1:T(8,128)(2,1)S(1)} %bitcast.111, bf16[1536,3072]{1,0:T(8,128)(2,1)} %param.16, f32[3072]{0:T(1024)S(1)} %bitcast.114, bf16[512,3072]{1,0:T(8,128)(2,1)S(1)} %bitcast.115), kind=kOutput, calls=%fused_computation.104 | convolution fusion | flops 4838129152 | bytes 20461568 | tf_op jit(solution)/shard_map/dot_general | solution.py:357
  188.9 0.8 multiply_reduce_fusion
  189.7 1.4 multiply_add_fusion
  191.3 0.6 collective-permute-start.6
  191.9 0.4 fusion.28
  192.2 0.8 copy.33
  193.1 2.3 %collective-permute-start.7 = (f32[1,34,64]{2,1,0:T(8,128)S(1)}, f32[1,34,64]{2,1,0:T(8,128)S(1)}, u32[]{:S(2)}, u32[]{:S(2)}) collective-permute-start(f32[1,34,64]{2,1,0:T(8,128)S(1)} %get-tuple-element.39), channel_id=1, source_target_pairs={{0,2},{2,4},{4,6},{1,3},{3,5},{5,7},{8,10},{10,12},{12,14},{9,11},... | collective-permute-start | bytes 26120 | tf_op jit(solution)/shard_map/ppermute | solution.py:32
  195.4 1.3 collective-permute-start.8
  196.7 0.4 fusion.17
  197.1 4.0 %collective-permute-done.8 = f32[1,34,64]{2,1,0:T(8,128)S(1)} collective-permute-done((f32[1,34,64]{2,1,0:T(8,128)S(1)}, f32[1,34,64]{2,1,0:T(8,128)S(1)}, u32[]{:S(2)}, u32[]{:S(2)}) %collective-permute-start.8) | collective-permute-done | bytes 8736 | tf_op jit(solution)/shard_map/ppermute | solution.py:34
  201.1 0.4 fusion.19
  201.5 0.4 fusion.21
  201.8 0.3 fusion.10
  202.2 0.4 fusion.12
  202.6 0.4 fusion.14
  202.9 0.4 fusion.5
  203.3 1.1 fusion.7
  (51 shorter events, 1.2 us)
Async XLA Ops:
  0.6 189.1 %copy-start = (bf16[3072,64]{0,1:T(8,128)(2,1)S(1)}, bf16[3072,64]{0,1:T(8,128)(2,1)}, u32[]{:S(2)}) copy-start(bf16[3072,64]{0,1:T(8,128)(2,1)} %param.17) | copy-start | bytes 1179652
  0.6 2.9 %copy-start.5 = (bf16[1,128,2,768]{3,2,1,0:T(2,128)(2,1)S(1)}, bf16[1,128,2,768]{3,2,1,0:T(2,128)(2,1)}, u32[]{:S(2)}) copy-start(bf16[1,128,2,768]{3,2,1,0:T(2,128)(2,1)} %param.12) | copy-start | bytes 1179652
  4.6 2.2 %copy-start.1 = (bf16[1,16,64,3,768]{4,2,1,3,0:T(8,128)(2,1)}, bf16[1,16,64,3,768]{4,2,1,3,0:T(8,128)(2,1)S(1)}, u32[]{:S(2)}) copy-start(bf16[1,16,64,3,768]{4,2,1,3,0:T(8,128)(2,1)S(1)} %copy.25) | copy-start | bytes 14155780
  6.7 1.8 copy-start.3
  8.5 82.7 %all-to-all-start = ((bf16[4,3328,128]{2,1,0:T(8,128)(2,1)}), bf16[4,3328,128]{2,1,0:T(8,128)(2,1)}, u32[]{:S(2)}, u32[]{:S(2)}) async-start(bf16[4,3328,128]{2,1,0:T(8,128)(2,1)} %copy-done.3), calls=%async_computation | async-start | bytes 6815744 | tf_op jit(solution)/shard_map/all_to_all | solution.py:226
  14.8 2.3 %copy-start.2 = (bf16[1,16,64,3,768]{4,2,1,3,0:T(8,128)(2,1)S(1)}, bf16[1,16,64,3,768]{4,2,1,3,0:T(8,128)(2,1)}, u32[]{:S(2)}) copy-start(bf16[1,16,64,3,768]{4,2,1,3,0:T(8,128)(2,1)} %copy-done.1) | copy-start | bytes 14155780
  17.8 2.6 %collective-permute-start = (bf16[2,1664,128]{2,1,0:T(8,128)(2,1)S(1)}, bf16[2,1664,128]{2,1,0:T(8,128)(2,1)}, u32[]{:S(2)}, u32[]{:S(2)}) collective-permute-start(bf16[2,1664,128]{2,1,0:T(8,128)(2,1)S(1)} %dynamic-slice_bitcast_fusion), channel_id=1, source_target_pairs={{0,1},{1,0},{2,3},{3,2},{4,5},{5,4},{6,7},{7,6},{8,9},{9,8},{10,11... | collective-permute-start | bytes 2555912 | tf_op jit(solution)/shard_map/ppermute | solution.py:251
  91.2 42.6 %all-to-all-start.1 = ((bf16[4,1664,128]{2,1,0:T(8,128)(2,1)}), bf16[4,1664,128]{2,1,0:T(8,128)(2,1)S(1)}, u32[]{:S(2)}, u32[]{:S(2)}) async-start(bf16[4,1664,128]{2,1,0:T(8,128)(2,1)} %pad_maximum_fusion), calls=%async_computation.1 | async-start | bytes 3407872 | tf_op jit(solution)/shard_map/all_to_all | solution.py:226
  135.0 5.0 %collective-permute-start.1 = (bf16[4,1152,128]{2,1,0:T(8,128)(2,1)}, bf16[4,1152,128]{2,1,0:T(8,128)(2,1)S(1)}, u32[]{:S(2)}, u32[]{:S(2)}) collective-permute-start(bf16[4,1152,128]{2,1,0:T(8,128)(2,1)} %slice.91), channel_id=1, source_target_pairs={{0,1},{1,0},{2,3},{3,2},{4,5},{5,4},{6,7},{7,6},{8,9},{9,8},{10,11... | collective-permute-start | bytes 3538952 | tf_op jit(solution)/shard_map/ppermute | solution.py:305
  135.0 37.0 %all-to-all-start.2 = ((bf16[4,1024,128]{2,1,0:T(8,128)(2,1)}), bf16[4,1024,128]{2,1,0:T(8,128)(2,1)}, u32[]{:S(2)}, u32[]{:S(2)}) async-start(bf16[4,1024,128]{2,1,0:T(8,128)(2,1)} %shard_map.132), calls=%async_computation.2 | async-start | bytes 2097152 | tf_op jit(solution)/shard_map/all_to_all | solution.py:226
  152.8 22.1 %copy-start.7 = (f32[1,16,32,64]{3,2,1,0:T(8,128)S(1)}, f32[1,16,32,64]{3,2,1,0:T(8,128)}, u32[]{:S(2)}) copy-start(f32[1,16,32,64]{3,2,1,0:T(8,128)} %param.18) | copy-start | bytes 393220
  152.8 22.3 %copy-start.10 = (f32[29]{0:T(128)S(1)}, f32[29]{0:T(128)}, u32[]{:S(2)}) copy-start(f32[29]{0:T(128)} %param.19) | copy-start | bytes 352
  153.5 23.4 %collective-permute-start.3 = (bf16[1,512,128]{2,1,0:T(8,128)(2,1)}, bf16[1,512,128]{2,1,0:T(8,128)(2,1)S(1)}, u32[]{:S(2)}, u32[]{:S(2)}) collective-permute-start(bf16[1,512,128]{2,1,0:T(8,128)(2,1)} %get-tuple-element.36), channel_id=1, source_target_pairs={{0,2},{2,4},{4,6},{6,0},{1,3},{3,5},{5,7},{7,1},{8,10},{10,12},{12... | collective-permute-start | bytes 393224 | tf_op jit(solution)/shard_map/ppermute | solution.py:236
  155.5 21.5 %collective-permute-start.4 = (bf16[1,512,128]{2,1,0:T(8,128)(2,1)S(1)}, bf16[1,512,128]{2,1,0:T(8,128)(2,1)S(1)}, u32[]{:S(2)}, u32[]{:S(2)}) collective-permute-start(bf16[1,512,128]{2,1,0:T(8,128)(2,1)S(1)} %get-tuple-element.35), channel_id=1, source_target_pairs={{0,4},{2,6},{4,0},{6,2},{1,5},{3,7},{5,1},{7,3},{8,12},{10,14},{12... | collective-permute-start | bytes 393224 | tf_op jit(solution)/shard_map/ppermute | solution.py:236
  157.8 19.1 %collective-permute-start.5 = (bf16[1,512,128]{2,1,0:T(8,128)(2,1)S(1)}, bf16[1,512,128]{2,1,0:T(8,128)(2,1)}, u32[]{:S(2)}, u32[]{:S(2)}) collective-permute-start(bf16[1,512,128]{2,1,0:T(8,128)(2,1)S(1)} %get-tuple-element.34), channel_id=1, source_target_pairs={{0,6},{2,0},{4,2},{6,4},{1,7},{3,1},{5,3},{7,5},{8,14},{10,8},{12,... | collective-permute-start | bytes 393224 | tf_op jit(solution)/shard_map/ppermute | solution.py:236
  173.5 5.2 %collective-permute-start.2 = (bf16[4,512,128]{1,2,0:T(8,128)(2,1)S(1)}, bf16[4,512,128]{1,2,0:T(8,128)(2,1)S(1)}, u32[]{:S(2)}, u32[]{:S(2)}) collective-permute-start(bf16[4,512,128]{1,2,0:T(8,128)(2,1)S(1)} %bitcast.108), channel_id=1, source_target_pairs={{0,1},{1,0},{2,3},{3,2},{4,5},{5,4},{6,7},{7,6},{8,9},{9,8},{10,11... | collective-permute-start | bytes 1572872 | tf_op jit(solution)/shard_map/ppermute | solution.py:251
  178.0 1.1 copy-start.9
  178.7 1.9 copy-start.11
  188.9 0.8 copy-start.8
  189.7 2.2 %copy-start.6 = (f32[3,3,64,64]{3,2,1,0:T(8,128)S(1)}, f32[3,3,64,64]{3,2,1,0:T(8,128)}, u32[]{:S(2)}) copy-start(f32[3,3,64,64]{3,2,1,0:T(8,128)} %param.21) | copy-start | bytes 442372
  191.3 12.0 %copy-start.4 = (f32[512,64]{1,0:T(8,128)}, f32[512,64]{1,0:T(8,128)S(1)}, u32[]{:S(2)}) copy-start(f32[512,64]{1,0:T(8,128)S(1)} %copy.35) | copy-start | bytes 393220
  191.3 1.8 collective-permute-start.6
  193.1 3.9 %collective-permute-start.7 = (f32[1,34,64]{2,1,0:T(8,128)S(1)}, f32[1,34,64]{2,1,0:T(8,128)S(1)}, u32[]{:S(2)}, u32[]{:S(2)}) collective-permute-start(f32[1,34,64]{2,1,0:T(8,128)S(1)} %get-tuple-element.39), channel_id=1, source_target_pairs={{0,2},{2,4},{4,6},{1,3},{3,5},{5,7},{8,10},{10,12},{12,14},{9,11},... | collective-permute-start | bytes 26120 | tf_op jit(solution)/shard_map/ppermute | solution.py:32
  195.4 5.7 %collective-permute-start.8 = (f32[1,34,64]{2,1,0:T(8,128)S(1)}, f32[1,34,64]{2,1,0:T(8,128)S(1)}, u32[]{:S(2)}, u32[]{:S(2)}) collective-permute-start(f32[1,34,64]{2,1,0:T(8,128)S(1)} %get-tuple-element.40), channel_id=1, source_target_pairs={{2,0},{4,2},{6,4},{3,1},{5,3},{7,5},{10,8},{12,10},{14,12},{11,9},... | collective-permute-start | bytes 26120 | tf_op jit(solution)/shard_map/ppermute | solution.py:34

commit v3 on v2

--- a/solution.py
+++ b/solution.py
@@ -184,40 +184,41 @@
                 at += text_half
 
 
-def pack_whole(img, txt, count, rows, halves, tile_cols):
+def pack_kernel(count, *args):
+    img_ref, txt_ref, whole_ref, halves_ref = args[-4:]
+
+    @pl.when(pl.program_id(0) < count)
+    def _():
+        pack_whole_kernel(*args[:-4], img_ref, txt_ref, whole_ref)
+
+    @pl.when(pl.program_id(0) >= count)
+    def _():
+        pack_halves_kernel(*args[:-4], img_ref, txt_ref, halves_ref)
+
+
+def pack(img, txt, count, heads, rows, halves, tile_cols):
     tokens, text_rows = img.shape[1], txt.shape[1]
     length = 3 * tokens + 2 * text_rows
     return pl.pallas_call(
-        functools.partial(pack_whole_kernel, rows, halves, tile_cols),
-        grid=(count,),
-        out_shape=jax.ShapeDtypeStruct((count, length, HD), img.dtype),
+        functools.partial(pack_kernel, count, rows, halves, tile_cols),
+        grid=(heads,),
+        out_shape=(
+            jax.ShapeDtypeStruct((count, length, HD), img.dtype),
+            jax.ShapeDtypeStruct((halves, heads - count, length // halves, HD), img.dtype),
+        ),
         in_specs=[
             pl.BlockSpec((3, tokens, HD), lambda i: (0, 0, i)),
             pl.BlockSpec((2, text_rows, HD), lambda i: (0, 0, i)),
         ],
-        out_specs=pl.BlockSpec((1, length, HD), lambda i: (i, 0, 0)),
+        out_specs=(
+            pl.BlockSpec((1, length, HD), lambda i: (jnp.minimum(i, count - 1), 0, 0)),
+            pl.BlockSpec(
+                (halves, 1, length // halves, HD), lambda i: (0, jnp.maximum(i - count, 0), 0, 0)
+            ),
+        ),
         compiler_params=pltpu.CompilerParams(vmem_limit_bytes=32 * 1024 * 1024),
         cost_estimate=pl.CostEstimate(
-            flops=0, bytes_accessed=4 * count * length * HD, transcendentals=0
-        ),
-    )(img, txt)
-
-
-def pack_halves(img, txt, first, count, rows, halves, tile_cols):
-    tokens, text_rows = img.shape[1], txt.shape[1]
-    length = (3 * tokens + 2 * text_rows) // halves
-    return pl.pallas_call(
-        functools.partial(pack_halves_kernel, rows, halves, tile_cols),
-        grid=(count,),
-        out_shape=jax.ShapeDtypeStruct((halves, count, length, HD), img.dtype),
-        in_specs=[
-            pl.BlockSpec((3, tokens, HD), lambda i: (0, 0, first + i)),
-            pl.BlockSpec((2, text_rows, HD), lambda i: (0, 0, first + i)),
-        ],
-        out_specs=pl.BlockSpec((halves, 1, length, HD), lambda i: (0, i, 0, 0)),
-        compiler_params=pltpu.CompilerParams(vmem_limit_bytes=32 * 1024 * 1024),
-        cost_estimate=pl.CostEstimate(
-            flops=0, bytes_accessed=4 * halves * count * length * HD, transcendentals=0
+            flops=0, bytes_accessed=4 * heads * length * HD, transcendentals=0
         ),
     )(img, txt)
 
@@ -265,10 +266,8 @@
 
     img = jnp.transpose(img_qkv[0].reshape(full, 3, heads * HD), (1, 0, 2))
     txt = jnp.transpose(txt_kv[0], (1, 0, 2))
-    send_a = pack_whole(img, txt, tiles, rows, halves, tile_cols)
-    send_a, img, txt = lax.optimization_barrier((send_a, img, txt))
+    send_a, send_b = pack(img, txt, tiles, heads, rows, halves, tile_cols)
     got_a = tile_mixed(send_a)
-    send_b = pack_halves(img, txt, tiles, heads - tiles, rows, halves, tile_cols)
     mixed_b = jnp.concatenate(col_swapped(send_b, me, 0), axis=0)
     mixed_b, got_a = lax.optimization_barrier((mixed_b, got_a))
     got_b = tile_mixed(mixed_b)
@@ -292,7 +291,7 @@
         moves_a.append((0, t, key + full, value + full, text_rows, image_all + t * text_rows))
     for s in range(halves):
         for t in range(tiles):
-            key = own if s == 0 else 0
+            key = own
             value = key + own + text_half
             slot = s * tiles + t
             moves_b.append((s, t, key, value, own, slot * own))
@@ -301,14 +300,19 @@
             )
     raw_a = attend(got_a, (), bias_a, full, tuple(moves_a), image_all, 512, 1024)
     raw_a, got_b = lax.optimization_barrier((raw_a, got_b))
-    out_a = tile_mixed(raw_a)
-    other_b = lax.ppermute(got_b[:, own:], "col", [(0, 1), (1, 0)])
+    out_a = lax.all_to_all(
+        raw_a.reshape(tiles * halves, own, HD),
+        ("tile", "col"),
+        split_axis=0,
+        concat_axis=0,
+        tiled=True,
+    ).reshape(tiles, halves, own, HD)
+    other_b = lax.ppermute(got_b, "col", [(0, 1), (1, 0)])
     raw_b = attend(got_b, (other_b,), bias_b, own, tuple(moves_b), image_all, 512, 1024)
     out_b = tile_stepped(raw_b)
     out_a, raw_b = lax.optimization_barrier((out_a, raw_b))
-    low, high = col_swapped(out_a.reshape(tiles, halves, own, HD), me, 1)
     third = heads - tiles
-    every = jnp.concatenate([low, out_b[:third], high, out_b[third:]], axis=0)
+    every = jnp.concatenate([out_a[:, 0], out_b[:third], out_a[:, 1], out_b[third:]], axis=0)
     return jnp.transpose(every, (1, 0, 2)).reshape(own, halves * heads * HD)
 
 

time: 205 us -> 200 us (0.976)
  local copies, waits for them, and re-layouts: 16.6 us -> 8.84 us
    all_to_all x3 -> x2, waiting for transfers between devices: 91.2 us -> 81.4 us  [tile_mixed(): lax.all_to_all(cells, 'tile', split_axis=0, concat_axis=0, tiled=True)]
    all_to_all x0 -> x1, waiting for transfers between devices: none -> 7.14 us  [by_heads(): lax.all_to_all(raw_a.reshape(tiles * halves, own, HD), ('tile', 'col'), s...]
    unnamed x29 -> x25, local copies, waits for them, and re-layouts: 10.8 us -> 5.04 us
    all_to_all x3 -> x2, starting transfers between devices: 14.1 us -> 9.89 us  [tile_mixed(): lax.all_to_all(cells, 'tile', split_axis=0, concat_axis=0, tiled=True)]
    all_to_all x0 -> x1, starting transfers between devices: none -> 3.56 us  [by_heads(): lax.all_to_all(raw_a.reshape(tiles * halves, own, HD), ('tile', 'col'), s...]
    ppermute x3, waiting for transfers between devices: 0.01 us -> 2.87 us  [tile_stepped(): lax.ppermute(block, 'tile', [(i, (i + step) % count) for i in range(count)])]
    ppermute x1, starting transfers between devices: 2.27 us -> 4.8 us  [padded_2(): lax.ppermute(tail, axis, [(i, (i + 1) % count) for i in range(ends)])]
    dynamic_slice x8 -> x0, local copies, waits for them, and re-layouts: 2.21 us -> none  [the longest x2 1.5 us: col_swapped(): kept = lax.dynamic_index_in_dim(cells, me, dim, keepdims=False)]
  transfers between devices with their start and end apart: 12 -> 11, of which waited for: 5 -> 6; matrix products, arithmetic and copies ran while one was open for 5% -> 4% of each run, Pallas kernels for 20% -> 21%
where the time goes in v3:
time: 200 us
  waiting for transfers between devices  97.9 us (49%)
  Pallas kernels  44 us (22%)
  starting transfers between devices  25.4 us (13%)
  matrix products  14.2 us (7%)
  local copies, waits for them, and re-layouts  8.84 us (4%)
  other arithmetic  5.99 us (3%)
  between operations  3.7 us (2%)
    all_to_all x2, waiting for transfers between devices, tile_mixed(): lax.all_to_all(cells, 'tile', split_axis=0, concat_axis=0, tiled=True)  81.4 us
    pallas_call x2, Pallas kernels, attend(): pl.pallas_call(functools.partial(attend_kernel, moves, key_chunk, image_k...  42.4 us
    all_to_all x2, starting transfers between devices, tile_mixed(): lax.all_to_all(cells, 'tile', split_axis=0, concat_axis=0, tiled=True)  9.89 us
    dot_general x1, matrix products, body(): branch = jnp.dot(attended, w_attn_out, preferred_element_type=jnp.float32)  8.8 us
    all_to_all x1, waiting for transfers between devices, by_heads(): lax.all_to_all(raw_a.reshape(tiles * halves, own, HD), ('tile', 'col'), s...  7.14 us
    ppermute x3, starting transfers between devices, tile_stepped(): lax.ppermute(block, 'tile', [(i, (i + step) % count) for i in range(count)])  5.7 us
    unnamed x25, local copies, waits for them, and re-layouts  5.04 us
    ppermute x1, starting transfers between devices, padded_2(): lax.ppermute(tail, axis, [(i, (i + 1) % count) for i in range(ends)])  4.8 us
  transfers between devices with their start and end apart: 11, of which 6 were waited for; matrix products, arithmetic and copies ran while one was open for 4% of the time, Pallas kernels for 21%

profile of v3, /device:TPU:0, one launch (start us, length us, event | category | flops | bytes accessed | tf_op | source)
XLA Modules:
  0.0 199.9 jit_solution(3620530361748023038)
XLA Ops:
  0.6 0.0 copy-start
  0.7 2.9 %copy.36 = bf16[1,16,64,3,768]{4,2,1,3,0:T(8,128)(2,1)S(1)} copy(bf16[1,16,64,3,768]{4,2,3,1,0:T(8,128)(2,1)} %param.11) | data formatting | bytes 9437184 | tf_op args[0]
  3.6 1.6 shard_map.130
  5.2 1.7 copy-done.1
  7.0 6.3 %all-to-all-start = ((bf16[4,3328,128]{2,1,0:T(8,128)(2,1)}), bf16[4,3328,128]{2,1,0:T(8,128)(2,1)}, u32[]{:S(2)}, u32[]{:S(2)}) async-start(bf16[4,3328,128]{2,1,0:T(8,128)(2,1)} %copy-done.1), calls=%async_computation | async-start | bytes 6815744 | tf_op jit(solution)/shard_map/all_to_all | solution.py:227
  13.3 0.1 dynamic-slice_bitcast_fusion
  13.3 0.1 collective-permute-start
  13.4 2.5 %collective-permute-done = bf16[2,1664,128]{2,1,0:T(8,128)(2,1)} collective-permute-done((bf16[2,1664,128]{2,1,0:T(8,128)(2,1)S(1)}, bf16[2,1664,128]{2,1,0:T(8,128)(2,1)}, u32[]{:S(2)}, u32[]{:S(2)}) %collective-permute-start) | collective-permute-done | bytes 852000 | tf_op jit(solution)/shard_map/ppermute | solution.py:252
  15.9 1.3 bitcast_select_fusion.1
  17.2 1.4 pad_maximum_fusion
  18.6 71.1 %all-to-all-done.q_ref.refs_0_ = bf16[4,3328,128]{2,1,0:T(8,128)(2,1)} async-done(((bf16[4,3328,128]{2,1,0:T(8,128)(2,1)}), bf16[4,3328,128]{2,1,0:T(8,128)(2,1)}, u32[]{:S(2)}, u32[]{:S(2)}) %all-to-all-start) | async-done | bytes 3407904 | tf_op jit(solution)/shard_map/all_to_all | solution.py:227
  89.7 3.6 %all-to-all-start.1 = ((bf16[4,1664,128]{2,1,0:T(8,128)(2,1)}), bf16[4,1664,128]{2,1,0:T(8,128)(2,1)S(1)}, u32[]{:S(2)}, u32[]{:S(2)}) async-start(bf16[4,1664,128]{2,1,0:T(8,128)(2,1)} %pad_maximum_fusion), calls=%async_computation.1 | async-start | bytes 3407872 | tf_op jit(solution)/shard_map/all_to_all | solution.py:227
  94.0 28.1 %shard_map.131 = bf16[4,1024,128]{2,1,0:T(8,128)(2,1)} custom-call(bf16[4,3328,128]{2,1,0:T(8,128)(2,1)} %all-to-all-done.q_ref.refs_0_, f32[1,512]{1,0:T(1,128)S(1)} %compare_select_fusion.2.bias_ref, bf16[4,3328,128]{2,1,0:T(8,128)(2,1)} %all-to-all-done.q_ref.refs_0_), custom_call_target="tpu_custom_call" | custom-call | flops 14495514624 | bytes 5505024 | tf_op jit(solution)/shard_map/pallas_call | solution.py:132
  122.1 10.3 %all-to-all-done.1.q_ref.refs_0_ = bf16[4,1664,128]{2,1,0:T(8,128)(2,1)S(1)} async-done(((bf16[4,1664,128]{2,1,0:T(8,128)(2,1)}), bf16[4,1664,128]{2,1,0:T(8,128)(2,1)S(1)}, u32[]{:S(2)}, u32[]{:S(2)}) %all-to-all-start.1) | async-done | bytes 1703968 | tf_op jit(solution)/shard_map/all_to_all | solution.py:227
  132.4 3.6 %all-to-all-start.2 = ((bf16[8,512,128]{2,1,0:T(8,128)(2,1)}), bf16[8,512,128]{2,1,0:T(8,128)(2,1)S(1)}, u32[]{:S(2)}, u32[]{:S(2)}) async-start(bf16[8,512,128]{2,1,0:T(8,128)(2,1)} %bitcast.10), calls=%async_computation.2 | async-start | bytes 2097152 | tf_op jit(solution)/shard_map/all_to_all | solution.py:303
  136.7 0.8 copy.41
  137.5 0.6 fusion.47
  139.4 1.4 dynamic-slice_add_fusion
  140.7 14.3 %shard_map.132 = bf16[4,512,128]{2,1,0:T(8,128)(2,1)S(1)} custom-call(bf16[4,1664,128]{2,1,0:T(8,128)(2,1)S(1)} %all-to-all-done.1.q_ref.refs_0_, f32[1,512]{1,0:T(1,128)S(1)} %compare_select_fusion.bias_ref, bf16[4,1664,128]{2,1,0:T(8,128)(2,1)S(1)} %all-to-all-done.1.q_ref.refs_0_, bf16[4,1664,128]{2,1,0:T(8,128)(2,1)} %collective-permute-done.1.refs_1_), custom_call_target="tpu_custom_call" | custom-call | flops 7247757312 | bytes 4456448 | tf_op jit(solution)/shard_map/pallas_call | solution.py:132
  155.0 0.7 constant_dynamic-slice_fusion.4
  155.7 1.9 collective-permute-start.2
  157.6 2.4 %collective-permute-start.3 = (bf16[1,512,128]{2,1,0:T(8,128)(2,1)S(1)}, bf16[1,512,128]{2,1,0:T(8,128)(2,1)}, u32[]{:S(2)}, u32[]{:S(2)}) collective-permute-start(bf16[1,512,128]{2,1,0:T(8,128)(2,1)S(1)} %get-tuple-element.27), channel_id=1, source_target_pairs={{0,4},{2,6},{4,0},{6,2},{1,5},{3,7},{5,1},{7,3},{8,12},{10,14},{12... | collective-permute-start | bytes 393224 | tf_op jit(solution)/shard_map/ppermute | solution.py:237
  160.0 1.4 collective-permute-start.4
  161.4 7.1 %all-to-all-done.2 = bf16[8,512,128]{2,1,0:T(8,128)(2,1)S(1)} async-done(((bf16[8,512,128]{2,1,0:T(8,128)(2,1)}), bf16[8,512,128]{2,1,0:T(8,128)(2,1)S(1)}, u32[]{:S(2)}, u32[]{:S(2)}) %all-to-all-start.2) | async-done | bytes 1048608 | tf_op jit(solution)/shard_map/all_to_all | solution.py:303
  168.6 2.9 %collective-permute-done.3 = bf16[1,512,128]{2,1,0:T(8,128)(2,1)} collective-permute-done((bf16[1,512,128]{2,1,0:T(8,128)(2,1)S(1)}, bf16[1,512,128]{2,1,0:T(8,128)(2,1)}, u32[]{:S(2)}, u32[]{:S(2)}) %collective-permute-start.3) | collective-permute-done | bytes 131104 | tf_op jit(solution)/shard_map/ppermute | solution.py:237
  171.5 1.0 pad_maximum_fusion.1
  172.6 0.1 bitcast_dynamic-update-slice_fusion
  172.7 0.7 copy.39
  173.4 8.8 %fusion.48 = (f32[512]{0:T(512)S(1)}, f32[512,3072]{1,0:T(8,128)S(1)}) fusion(bf16[512,1536]{0,1:T(8,128)(2,1)S(1)} %bitcast.107, bf16[1536,3072]{1,0:T(8,128)(2,1)} %param.16, f32[3072]{0:T(1024)} %bitcast.112, bf16[512,3072]{1,0:T(8,128)(2,1)} %bitcast.113), kind=kOutput, calls=%fused_computation.97 | convolution fusion | flops 4838129152 | bytes 20461568 | tf_op jit(solution)/shard_map/dot_general | solution.py:361
  182.3 0.8 multiply_reduce_fusion
  183.1 0.1 copy-done.6
  183.2 1.4 multiply_add_fusion
  184.6 0.1 copy.42
  184.8 0.1 collective-permute-start.5
  184.9 0.4 fusion.27
  185.2 0.8 copy.40
  186.1 4.8 %collective-permute-start.6 = (f32[1,34,64]{2,1,0:T(8,128)S(1)}, f32[1,34,64]{2,1,0:T(8,128)S(1)}, u32[]{:S(2)}, u32[]{:S(2)}) collective-permute-start(f32[1,34,64]{2,1,0:T(8,128)S(1)} %get-tuple-element.31), channel_id=1, source_target_pairs={{0,2},{2,4},{4,6},{1,3},{3,5},{5,7},{8,10},{10,12},{12,14},{9,11},... | collective-permute-start | bytes 26120 | tf_op jit(solution)/shard_map/ppermute | solution.py:32
  190.9 1.3 collective-permute-start.7
  192.2 0.4 fusion.16
  192.6 4.0 %collective-permute-done.7 = f32[1,34,64]{2,1,0:T(8,128)S(1)} collective-permute-done((f32[1,34,64]{2,1,0:T(8,128)S(1)}, f32[1,34,64]{2,1,0:T(8,128)S(1)}, u32[]{:S(2)}, u32[]{:S(2)}) %collective-permute-start.7) | collective-permute-done | bytes 8736 | tf_op jit(solution)/shard_map/ppermute | solution.py:34
  196.6 0.1 maximum_maximum_fusion
  196.6 0.4 fusion.18
  197.0 0.3 fusion.20
  197.4 0.4 fusion.11
  197.7 0.4 fusion.13
  198.1 0.4 fusion.9
  198.4 0.4 fusion.5
  198.8 1.1 fusion.7
  (34 shorter events, 0.3 us)
Async XLA Ops:
  0.6 182.4 %copy-start = (bf16[3072,64]{0,1:T(8,128)(2,1)S(1)}, bf16[3072,64]{0,1:T(8,128)(2,1)}, u32[]{:S(2)}) copy-start(bf16[3072,64]{0,1:T(8,128)(2,1)} %param.17) | copy-start | bytes 1179652
  0.6 2.9 %copy-start.3 = (bf16[1,128,2,768]{3,2,1,0:T(2,128)(2,1)S(1)}, bf16[1,128,2,768]{3,2,1,0:T(2,128)(2,1)}, u32[]{:S(2)}) copy-start(bf16[1,128,2,768]{3,2,1,0:T(2,128)(2,1)} %param.12) | copy-start | bytes 1179652
  5.2 1.7 copy-start.1
  7.0 82.7 %all-to-all-start = ((bf16[4,3328,128]{2,1,0:T(8,128)(2,1)}), bf16[4,3328,128]{2,1,0:T(8,128)(2,1)}, u32[]{:S(2)}, u32[]{:S(2)}) async-start(bf16[4,3328,128]{2,1,0:T(8,128)(2,1)} %copy-done.1), calls=%async_computation | async-start | bytes 6815744 | tf_op jit(solution)/shard_map/all_to_all | solution.py:227
  13.3 2.6 %collective-permute-start = (bf16[2,1664,128]{2,1,0:T(8,128)(2,1)S(1)}, bf16[2,1664,128]{2,1,0:T(8,128)(2,1)}, u32[]{:S(2)}, u32[]{:S(2)}) collective-permute-start(bf16[2,1664,128]{2,1,0:T(8,128)(2,1)S(1)} %dynamic-slice_bitcast_fusion), channel_id=1, source_target_pairs={{0,1},{1,0},{2,3},{3,2},{4,5},{5,4},{6,7},{7,6},{8,9},{9,8},{10,11... | collective-permute-start | bytes 2555912 | tf_op jit(solution)/shard_map/ppermute | solution.py:252
  89.7 42.7 %all-to-all-start.1 = ((bf16[4,1664,128]{2,1,0:T(8,128)(2,1)}), bf16[4,1664,128]{2,1,0:T(8,128)(2,1)S(1)}, u32[]{:S(2)}, u32[]{:S(2)}) async-start(bf16[4,1664,128]{2,1,0:T(8,128)(2,1)} %pad_maximum_fusion), calls=%async_computation.1 | async-start | bytes 3407872 | tf_op jit(solution)/shard_map/all_to_all | solution.py:227
  93.9 42.7 %copy-start.5 = (f32[1,16,32,64]{3,2,1,0:T(8,128)S(1)}, f32[1,16,32,64]{3,2,1,0:T(8,128)}, u32[]{:S(2)}) copy-start(f32[1,16,32,64]{3,2,1,0:T(8,128)} %param.18) | copy-start | bytes 393220
  93.9 43.5 %copy-start.8 = (f32[29]{0:T(128)S(1)}, f32[29]{0:T(128)}, u32[]{:S(2)}) copy-start(f32[29]{0:T(128)} %param.19) | copy-start | bytes 352
  132.4 8.3 %collective-permute-start.1 = (bf16[4,1664,128]{2,1,0:T(8,128)(2,1)S(1)}, bf16[4,1664,128]{2,1,0:T(8,128)(2,1)}, u32[]{:S(2)}, u32[]{:S(2)}) collective-permute-start(bf16[4,1664,128]{2,1,0:T(8,128)(2,1)S(1)} %all-to-all-done.1.q_ref.refs_0_), channel_id=1, source_target_pairs={{0,1},{1,0},{2,3},{3,2},{4,5},{5,4},{6,7},{7,6},{8,9},{9,8},{10,11... | collective-permute-start | bytes 5111816 | tf_op jit(solution)/shard_map/ppermute | solution.py:310
  132.4 36.2 %all-to-all-start.2 = ((bf16[8,512,128]{2,1,0:T(8,128)(2,1)}), bf16[8,512,128]{2,1,0:T(8,128)(2,1)S(1)}, u32[]{:S(2)}, u32[]{:S(2)}) async-start(bf16[8,512,128]{2,1,0:T(8,128)(2,1)} %bitcast.10), calls=%async_computation.2 | async-start | bytes 2097152 | tf_op jit(solution)/shard_map/all_to_all | solution.py:303
  155.7 12.9 %collective-permute-start.2 = (bf16[1,512,128]{2,1,0:T(8,128)(2,1)}, bf16[1,512,128]{2,1,0:T(8,128)(2,1)S(1)}, u32[]{:S(2)}, u32[]{:S(2)}) collective-permute-start(bf16[1,512,128]{2,1,0:T(8,128)(2,1)} %get-tuple-element.28), channel_id=1, source_target_pairs={{0,2},{2,4},{4,6},{6,0},{1,3},{3,5},{5,7},{7,1},{8,10},{10,12},{12... | collective-permute-start | bytes 393224 | tf_op jit(solution)/shard_map/ppermute | solution.py:237
  157.6 13.9 %collective-permute-start.3 = (bf16[1,512,128]{2,1,0:T(8,128)(2,1)S(1)}, bf16[1,512,128]{2,1,0:T(8,128)(2,1)}, u32[]{:S(2)}, u32[]{:S(2)}) collective-permute-start(bf16[1,512,128]{2,1,0:T(8,128)(2,1)S(1)} %get-tuple-element.27), channel_id=1, source_target_pairs={{0,4},{2,6},{4,0},{6,2},{1,5},{3,7},{5,1},{7,3},{8,12},{10,14},{12... | collective-permute-start | bytes 393224 | tf_op jit(solution)/shard_map/ppermute | solution.py:237
  160.0 11.5 %collective-permute-start.4 = (bf16[1,512,128]{2,1,0:T(8,128)(2,1)S(1)}, bf16[1,512,128]{2,1,0:T(8,128)(2,1)}, u32[]{:S(2)}, u32[]{:S(2)}) collective-permute-start(bf16[1,512,128]{2,1,0:T(8,128)(2,1)S(1)} %get-tuple-element.26), channel_id=1, source_target_pairs={{0,6},{2,0},{4,2},{6,4},{1,7},{3,1},{5,3},{7,5},{8,14},{10,8},{12,... | collective-permute-start | bytes 393224 | tf_op jit(solution)/shard_map/ppermute | solution.py:237
  182.3 0.9 copy-start.6
  182.3 0.9 copy-start.7
  183.2 1.7 copy-start.4
  184.7 14.1 %copy-start.2 = (f32[512,64]{1,0:T(8,128)}, f32[512,64]{1,0:T(8,128)S(1)}, u32[]{:S(2)}) copy-start(f32[512,64]{1,0:T(8,128)S(1)} %copy.42) | copy-start | bytes 393220
  184.8 1.3 collective-permute-start.5
  186.1 6.5 %collective-permute-start.6 = (f32[1,34,64]{2,1,0:T(8,128)S(1)}, f32[1,34,64]{2,1,0:T(8,128)S(1)}, u32[]{:S(2)}, u32[]{:S(2)}) collective-permute-start(f32[1,34,64]{2,1,0:T(8,128)S(1)} %get-tuple-element.31), channel_id=1, source_target_pairs={{0,2},{2,4},{4,6},{1,3},{3,5},{5,7},{8,10},{10,12},{12,14},{9,11},... | collective-permute-start | bytes 26120 | tf_op jit(solution)/shard_map/ppermute | solution.py:32
  190.9 5.7 %collective-permute-start.7 = (f32[1,34,64]{2,1,0:T(8,128)S(1)}, f32[1,34,64]{2,1,0:T(8,128)S(1)}, u32[]{:S(2)}, u32[]{:S(2)}) collective-permute-start(f32[1,34,64]{2,1,0:T(8,128)S(1)} %get-tuple-element.32), channel_id=1, source_target_pairs={{2,0},{4,2},{6,4},{3,1},{5,3},{7,5},{10,8},{12,10},{14,12},{11,9},... | collective-permute-start | bytes 26120 | tf_op jit(solution)/shard_map/ppermute | solution.py:34
